TPU v7x, 256 devices: a whole 4x4x8 slice. The times are simulated.
256 devices in a mesh: blk: 16 (over y_hi, x, core), row: 16 (over y_lo, z).
Axes of the slice: x: 4, y: 4 (y_hi: 2, y_lo: 2; y = y_hi * 2 + y_lo), z: 8, core: 2. Of those that a mesh axis runs over, the one named last changes fastest.
Arguments:
- images: float32 [16384, 1152], P(('blk', 'row')), may hold values from -0.2 to 0.2
- texts: float32 [16384, 1152], P(('blk', 'row')), may hold values from -0.2 to 0.2
- scale: float32 [1], replicated, may hold values from 4 to 12
- bias: float32 [1], replicated, may hold values from -3 to -1
Outputs:
- image_grad: float32 [16384, 1152], P(('blk', 'row'))
- text_grad: float32 [16384, 1152], P(('blk', 'row'))
All inputs are finite; a program needn't handle non-finite values.
Results may differ from a plain program's by a relative error of at most 0.0053.
Values may be sent and summed in bfloat16 or wider, within the bound.
A program may use at most 64 MiB of HBM per device.

v0:
```python
import jax
import jax.numpy as jnp
from jax import lax
from jax.sharding import PartitionSpec as P

EPS = 1e-06


def from_behind(x, axis, by):
    peers = lax.axis_size(axis)
    return lax.ppermute(x, axis, [(i, (i + by) % peers) for i in range(peers)])


def normalize(values):
    norm_rows = jnp.sqrt(jnp.sum(values * values, axis=1, keepdims=True) + EPS)
    return (values / norm_rows, norm_rows)


def project_back(grad_hat, unit_rows, norm_rows):
    return (grad_hat - unit_rows * jnp.sum(unit_rows * grad_hat, axis=1, keepdims=True)) / norm_rows


def tile_terms(group_images, text_tile, positive, scale_value, bias_value):
    logits = (
        scale_value
        * jnp.einsum("id,jd->ij", group_images, text_tile, preferred_element_type=jnp.float32)
        + bias_value
    )
    sign = jnp.where(positive, 1.0, -1.0).astype(jnp.float32)
    coef = (-scale_value * sign * jax.nn.sigmoid(-sign * logits)).astype(jnp.bfloat16)
    image_part = jnp.dot(coef, text_tile, preferred_element_type=jnp.float32)
    text_part = jnp.einsum("ij,id->jd", coef, group_images, preferred_element_type=jnp.float32)
    return (image_part, text_part)


def body(images, texts, scale, bias):
    groups = lax.axis_size("blk")
    row_id = lax.axis_index("row")
    rows_here = images.shape[0]
    width = images.shape[1]
    scale_value = scale[0]
    bias_value = bias[0]
    image_unit, image_norm = normalize(images)
    text_unit, text_norm = normalize(texts)
    image_hat = image_unit.astype(jnp.bfloat16)
    text_hat = text_unit.astype(jnp.bfloat16)
    group_images = lax.all_gather(image_hat, "row", axis=0, tiled=True)
    group_rows = group_images.shape[0]
    image_pos = jnp.arange(group_rows, dtype=jnp.int32)
    image_start = jnp.zeros((group_rows, width), jnp.float32)
    text_pos = jnp.arange(rows_here, dtype=jnp.int32)

    def absorb(turn_index, text_tile, partial_value, image_acc):
        positive = jnp.logical_and(
            turn_index == 0, image_pos[:, None] == row_id * rows_here + text_pos[None, :]
        )
        image_part, text_part = tile_terms(
            group_images, text_tile, positive, scale_value, bias_value
        )
        return (partial_value + text_part, image_acc + image_part)

    def pass_partial(partial_value):
        return from_behind(partial_value, "blk", 1)

    def cycle_turn(turn_index, carry):
        text_tile, partial_value, image_acc = carry
        partial_value, image_acc = absorb(turn_index, text_tile, partial_value, image_acc)
        partial_value = pass_partial(partial_value)
        text_tile = from_behind(text_tile, "blk", 1)
        return (text_tile, partial_value, image_acc)

    start_carry = (text_hat, jnp.zeros((rows_here, width), jnp.float32), image_start)
    text_tile, partial_value, image_acc = lax.fori_loop(0, groups - 1, cycle_turn, start_carry)
    partial_value, image_acc = absorb(groups - 1, text_tile, partial_value, image_acc)
    text_hat_grad = pass_partial(partial_value)
    image_hat_grad = lax.psum_scatter(image_acc, "row", scatter_dimension=0, tiled=True)
    image_grad = project_back(image_hat_grad, image_unit, image_norm)
    text_grad = project_back(text_hat_grad, text_unit, text_norm)
    return (image_grad, text_grad)


def solution(mesh):
    placed = (P(("blk", "row"), None), P(("blk", "row"), None), P(), P())
    return jax.shard_map(
        body,
        mesh=mesh,
        in_specs=placed,
        out_specs=(P(("blk", "row"), None), P(("blk", "row"), None)),
        check_vma=False,
    )
```

profile of v0, /device:TPU:8, one launch (start us, length us, event | category | flops | bytes accessed | tf_op | source)
XLA Modules:
  0.0 398.6 jit_solution(1306981986876402427)
XLA Ops:
  13.6 71.0 %all-gather.2.cloned.1.call-done = bf16[1024,1152]{1,0:T(8,128)(2,1)} async-done(((bf16[64,1152]{1,0:T(8,128)(2,1)}), bf16[1024,1152]{1,0:T(8,128)(2,1)}) %all-gather.2.cloned.1.call-update) | async-done | bytes 2359312 | tf_op jit(solution)/shard_map/all_gather | solution.py:47
  84.6 217.4 %while.20 = (s32[]{:T(128)}, bf16[64,1152]{1,0:T(8,128)(2,1)S(1)}, f32[64,1152]{1,0:T(8,128)S(1)}, f32[1024,1152]{1,0:T(8,128)}, f32[]{:T(128)}, /*index=5*/s32[...) while((s32[]{:T(128)}, bf16[64,1152]{1,0:T(8,128)(2,1)S(1)}, ...), condition=%wide.region_3.4_spmd.clone, body=%wide.region_2.3_spmd.clone.sunk | while | flops 456269888 | bytes 26936052 | solution.py:73
  93.7 5.4 %collective-permute-done.1 = f32[64,1152]{1,0:T(8,128)S(1)} collective-permute-done((f32[64,1152]{1,0:T(8,128)S(1)}, f32[64,1152]{1,0:T(8,128)S(1)}, u32[]{:S(2)}, u32[]{:S(2)}) %collective-permute-start.1) | collective-permute-done | bytes 294944 | tf_op jit(solution)/shard_map/while/body/eval_jaxpr/ppermute | solution.py:11
  99.3 4.0 fusion.47
  103.9 5.3 %convolution_add_fusion.7 = f32[1024,1152]{1,0:T(8,128)} fusion(bf16[1024,64]{0,1:T(8,128)(2,1)S(1)} %fusion.47, bf16[64,1152]{1,0:T(8,128)(2,1)S(1)} %copy.11, f32[1024,1152]{1,0:T(8,128)} %get-tuple-element.367, pred[]{:T(512)S(6)} %eq.66), kind=kOutput, calls=%fused_computation.2.clone.1 | convolution fusion | flops 153354240 | bytes 9715713 | tf_op jit(solution)/shard_map/while/body/eval_jaxpr/dot_general | solution.py:31
  109.2 4.5 %collective-permute-done.1 = f32[64,1152]{1,0:T(8,128)S(1)} collective-permute-done((f32[64,1152]{1,0:T(8,128)S(1)}, f32[64,1152]{1,0:T(8,128)S(1)}, u32[]{:S(2)}, u32[]{:S(2)}) %collective-permute-start.1) | collective-permute-done | bytes 294944 | tf_op jit(solution)/shard_map/while/body/eval_jaxpr/ppermute | solution.py:11
  113.8 4.0 fusion.47
  118.4 5.3 %convolution_add_fusion.7 = f32[1024,1152]{1,0:T(8,128)} fusion(bf16[1024,64]{0,1:T(8,128)(2,1)S(1)} %fusion.47, bf16[64,1152]{1,0:T(8,128)(2,1)S(1)} %copy.11, f32[1024,1152]{1,0:T(8,128)} %get-tuple-element.367, pred[]{:T(512)S(6)} %eq.66), kind=kOutput, calls=%fused_computation.2.clone.1 | convolution fusion | flops 153354240 | bytes 9715713 | tf_op jit(solution)/shard_map/while/body/eval_jaxpr/dot_general | solution.py:31
  123.7 4.5 %collective-permute-done.1 = f32[64,1152]{1,0:T(8,128)S(1)} collective-permute-done((f32[64,1152]{1,0:T(8,128)S(1)}, f32[64,1152]{1,0:T(8,128)S(1)}, u32[]{:S(2)}, u32[]{:S(2)}) %collective-permute-start.1) | collective-permute-done | bytes 294944 | tf_op jit(solution)/shard_map/while/body/eval_jaxpr/ppermute | solution.py:11
  128.2 4.0 fusion.47
  132.9 5.3 %convolution_add_fusion.7 = f32[1024,1152]{1,0:T(8,128)} fusion(bf16[1024,64]{0,1:T(8,128)(2,1)S(1)} %fusion.47, bf16[64,1152]{1,0:T(8,128)(2,1)S(1)} %copy.11, f32[1024,1152]{1,0:T(8,128)} %get-tuple-element.367, pred[]{:T(512)S(6)} %eq.66), kind=kOutput, calls=%fused_computation.2.clone.1 | convolution fusion | flops 153354240 | bytes 9715713 | tf_op jit(solution)/shard_map/while/body/eval_jaxpr/dot_general | solution.py:31
  138.2 4.5 %collective-permute-done.1 = f32[64,1152]{1,0:T(8,128)S(1)} collective-permute-done((f32[64,1152]{1,0:T(8,128)S(1)}, f32[64,1152]{1,0:T(8,128)S(1)}, u32[]{:S(2)}, u32[]{:S(2)}) %collective-permute-start.1) | collective-permute-done | bytes 294944 | tf_op jit(solution)/shard_map/while/body/eval_jaxpr/ppermute | solution.py:11
  142.7 4.0 fusion.47
  147.4 5.3 %convolution_add_fusion.7 = f32[1024,1152]{1,0:T(8,128)} fusion(bf16[1024,64]{0,1:T(8,128)(2,1)S(1)} %fusion.47, bf16[64,1152]{1,0:T(8,128)(2,1)S(1)} %copy.11, f32[1024,1152]{1,0:T(8,128)} %get-tuple-element.367, pred[]{:T(512)S(6)} %eq.66), kind=kOutput, calls=%fused_computation.2.clone.1 | convolution fusion | flops 153354240 | bytes 9715713 | tf_op jit(solution)/shard_map/while/body/eval_jaxpr/dot_general | solution.py:31
  152.6 4.5 %collective-permute-done.1 = f32[64,1152]{1,0:T(8,128)S(1)} collective-permute-done((f32[64,1152]{1,0:T(8,128)S(1)}, f32[64,1152]{1,0:T(8,128)S(1)}, u32[]{:S(2)}, u32[]{:S(2)}) %collective-permute-start.1) | collective-permute-done | bytes 294944 | tf_op jit(solution)/shard_map/while/body/eval_jaxpr/ppermute | solution.py:11
  157.2 4.0 fusion.47
  161.9 5.3 %convolution_add_fusion.7 = f32[1024,1152]{1,0:T(8,128)} fusion(bf16[1024,64]{0,1:T(8,128)(2,1)S(1)} %fusion.47, bf16[64,1152]{1,0:T(8,128)(2,1)S(1)} %copy.11, f32[1024,1152]{1,0:T(8,128)} %get-tuple-element.367, pred[]{:T(512)S(6)} %eq.66), kind=kOutput, calls=%fused_computation.2.clone.1 | convolution fusion | flops 153354240 | bytes 9715713 | tf_op jit(solution)/shard_map/while/body/eval_jaxpr/dot_general | solution.py:31
  167.1 4.5 %collective-permute-done.1 = f32[64,1152]{1,0:T(8,128)S(1)} collective-permute-done((f32[64,1152]{1,0:T(8,128)S(1)}, f32[64,1152]{1,0:T(8,128)S(1)}, u32[]{:S(2)}, u32[]{:S(2)}) %collective-permute-start.1) | collective-permute-done | bytes 294944 | tf_op jit(solution)/shard_map/while/body/eval_jaxpr/ppermute | solution.py:11
  171.7 4.0 fusion.47
  176.3 5.3 %convolution_add_fusion.7 = f32[1024,1152]{1,0:T(8,128)} fusion(bf16[1024,64]{0,1:T(8,128)(2,1)S(1)} %fusion.47, bf16[64,1152]{1,0:T(8,128)(2,1)S(1)} %copy.11, f32[1024,1152]{1,0:T(8,128)} %get-tuple-element.367, pred[]{:T(512)S(6)} %eq.66), kind=kOutput, calls=%fused_computation.2.clone.1 | convolution fusion | flops 153354240 | bytes 9715713 | tf_op jit(solution)/shard_map/while/body/eval_jaxpr/dot_general | solution.py:31
  181.6 4.5 %collective-permute-done.1 = f32[64,1152]{1,0:T(8,128)S(1)} collective-permute-done((f32[64,1152]{1,0:T(8,128)S(1)}, f32[64,1152]{1,0:T(8,128)S(1)}, u32[]{:S(2)}, u32[]{:S(2)}) %collective-permute-start.1) | collective-permute-done | bytes 294944 | tf_op jit(solution)/shard_map/while/body/eval_jaxpr/ppermute | solution.py:11
  186.2 4.0 fusion.47
  190.8 5.3 %convolution_add_fusion.7 = f32[1024,1152]{1,0:T(8,128)} fusion(bf16[1024,64]{0,1:T(8,128)(2,1)S(1)} %fusion.47, bf16[64,1152]{1,0:T(8,128)(2,1)S(1)} %copy.11, f32[1024,1152]{1,0:T(8,128)} %get-tuple-element.367, pred[]{:T(512)S(6)} %eq.66), kind=kOutput, calls=%fused_computation.2.clone.1 | convolution fusion | flops 153354240 | bytes 9715713 | tf_op jit(solution)/shard_map/while/body/eval_jaxpr/dot_general | solution.py:31
  196.1 4.5 %collective-permute-done.1 = f32[64,1152]{1,0:T(8,128)S(1)} collective-permute-done((f32[64,1152]{1,0:T(8,128)S(1)}, f32[64,1152]{1,0:T(8,128)S(1)}, u32[]{:S(2)}, u32[]{:S(2)}) %collective-permute-start.1) | collective-permute-done | bytes 294944 | tf_op jit(solution)/shard_map/while/body/eval_jaxpr/ppermute | solution.py:11
  200.7 4.0 fusion.47
  205.3 5.3 %convolution_add_fusion.7 = f32[1024,1152]{1,0:T(8,128)} fusion(bf16[1024,64]{0,1:T(8,128)(2,1)S(1)} %fusion.47, bf16[64,1152]{1,0:T(8,128)(2,1)S(1)} %copy.11, f32[1024,1152]{1,0:T(8,128)} %get-tuple-element.367, pred[]{:T(512)S(6)} %eq.66), kind=kOutput, calls=%fused_computation.2.clone.1 | convolution fusion | flops 153354240 | bytes 9715713 | tf_op jit(solution)/shard_map/while/body/eval_jaxpr/dot_general | solution.py:31
  210.6 4.5 %collective-permute-done.1 = f32[64,1152]{1,0:T(8,128)S(1)} collective-permute-done((f32[64,1152]{1,0:T(8,128)S(1)}, f32[64,1152]{1,0:T(8,128)S(1)}, u32[]{:S(2)}, u32[]{:S(2)}) %collective-permute-start.1) | collective-permute-done | bytes 294944 | tf_op jit(solution)/shard_map/while/body/eval_jaxpr/ppermute | solution.py:11
  215.2 4.0 fusion.47
  219.8 5.3 %convolution_add_fusion.7 = f32[1024,1152]{1,0:T(8,128)} fusion(bf16[1024,64]{0,1:T(8,128)(2,1)S(1)} %fusion.47, bf16[64,1152]{1,0:T(8,128)(2,1)S(1)} %copy.11, f32[1024,1152]{1,0:T(8,128)} %get-tuple-element.367, pred[]{:T(512)S(6)} %eq.66), kind=kOutput, calls=%fused_computation.2.clone.1 | convolution fusion | flops 153354240 | bytes 9715713 | tf_op jit(solution)/shard_map/while/body/eval_jaxpr/dot_general | solution.py:31
  225.1 4.5 %collective-permute-done.1 = f32[64,1152]{1,0:T(8,128)S(1)} collective-permute-done((f32[64,1152]{1,0:T(8,128)S(1)}, f32[64,1152]{1,0:T(8,128)S(1)}, u32[]{:S(2)}, u32[]{:S(2)}) %collective-permute-start.1) | collective-permute-done | bytes 294944 | tf_op jit(solution)/shard_map/while/body/eval_jaxpr/ppermute | solution.py:11
  229.7 4.0 fusion.47
  234.3 5.3 %convolution_add_fusion.7 = f32[1024,1152]{1,0:T(8,128)} fusion(bf16[1024,64]{0,1:T(8,128)(2,1)S(1)} %fusion.47, bf16[64,1152]{1,0:T(8,128)(2,1)S(1)} %copy.11, f32[1024,1152]{1,0:T(8,128)} %get-tuple-element.367, pred[]{:T(512)S(6)} %eq.66), kind=kOutput, calls=%fused_computation.2.clone.1 | convolution fusion | flops 153354240 | bytes 9715713 | tf_op jit(solution)/shard_map/while/body/eval_jaxpr/dot_general | solution.py:31
  239.6 4.5 %collective-permute-done.1 = f32[64,1152]{1,0:T(8,128)S(1)} collective-permute-done((f32[64,1152]{1,0:T(8,128)S(1)}, f32[64,1152]{1,0:T(8,128)S(1)}, u32[]{:S(2)}, u32[]{:S(2)}) %collective-permute-start.1) | collective-permute-done | bytes 294944 | tf_op jit(solution)/shard_map/while/body/eval_jaxpr/ppermute | solution.py:11
  244.2 4.0 fusion.47
  248.8 5.3 %convolution_add_fusion.7 = f32[1024,1152]{1,0:T(8,128)} fusion(bf16[1024,64]{0,1:T(8,128)(2,1)S(1)} %fusion.47, bf16[64,1152]{1,0:T(8,128)(2,1)S(1)} %copy.11, f32[1024,1152]{1,0:T(8,128)} %get-tuple-element.367, pred[]{:T(512)S(6)} %eq.66), kind=kOutput, calls=%fused_computation.2.clone.1 | convolution fusion | flops 153354240 | bytes 9715713 | tf_op jit(solution)/shard_map/while/body/eval_jaxpr/dot_general | solution.py:31
  254.1 4.5 %collective-permute-done.1 = f32[64,1152]{1,0:T(8,128)S(1)} collective-permute-done((f32[64,1152]{1,0:T(8,128)S(1)}, f32[64,1152]{1,0:T(8,128)S(1)}, u32[]{:S(2)}, u32[]{:S(2)}) %collective-permute-start.1) | collective-permute-done | bytes 294944 | tf_op jit(solution)/shard_map/while/body/eval_jaxpr/ppermute | solution.py:11
  258.7 4.0 fusion.47
  263.3 5.3 %convolution_add_fusion.7 = f32[1024,1152]{1,0:T(8,128)} fusion(bf16[1024,64]{0,1:T(8,128)(2,1)S(1)} %fusion.47, bf16[64,1152]{1,0:T(8,128)(2,1)S(1)} %copy.11, f32[1024,1152]{1,0:T(8,128)} %get-tuple-element.367, pred[]{:T(512)S(6)} %eq.66), kind=kOutput, calls=%fused_computation.2.clone.1 | convolution fusion | flops 153354240 | bytes 9715713 | tf_op jit(solution)/shard_map/while/body/eval_jaxpr/dot_general | solution.py:31
  268.6 4.5 %collective-permute-done.1 = f32[64,1152]{1,0:T(8,128)S(1)} collective-permute-done((f32[64,1152]{1,0:T(8,128)S(1)}, f32[64,1152]{1,0:T(8,128)S(1)}, u32[]{:S(2)}, u32[]{:S(2)}) %collective-permute-start.1) | collective-permute-done | bytes 294944 | tf_op jit(solution)/shard_map/while/body/eval_jaxpr/ppermute | solution.py:11
  273.2 4.0 fusion.47
  277.8 5.3 %convolution_add_fusion.7 = f32[1024,1152]{1,0:T(8,128)} fusion(bf16[1024,64]{0,1:T(8,128)(2,1)S(1)} %fusion.47, bf16[64,1152]{1,0:T(8,128)(2,1)S(1)} %copy.11, f32[1024,1152]{1,0:T(8,128)} %get-tuple-element.367, pred[]{:T(512)S(6)} %eq.66), kind=kOutput, calls=%fused_computation.2.clone.1 | convolution fusion | flops 153354240 | bytes 9715713 | tf_op jit(solution)/shard_map/while/body/eval_jaxpr/dot_general | solution.py:31
  283.1 4.5 %collective-permute-done.1 = f32[64,1152]{1,0:T(8,128)S(1)} collective-permute-done((f32[64,1152]{1,0:T(8,128)S(1)}, f32[64,1152]{1,0:T(8,128)S(1)}, u32[]{:S(2)}, u32[]{:S(2)}) %collective-permute-start.1) | collective-permute-done | bytes 294944 | tf_op jit(solution)/shard_map/while/body/eval_jaxpr/ppermute | solution.py:11
  287.7 4.0 fusion.47
  292.3 5.3 %convolution_add_fusion.7 = f32[1024,1152]{1,0:T(8,128)} fusion(bf16[1024,64]{0,1:T(8,128)(2,1)S(1)} %fusion.47, bf16[64,1152]{1,0:T(8,128)(2,1)S(1)} %copy.11, f32[1024,1152]{1,0:T(8,128)} %get-tuple-element.367, pred[]{:T(512)S(6)} %eq.66), kind=kOutput, calls=%fused_computation.2.clone.1 | convolution fusion | flops 153354240 | bytes 9715713 | tf_op jit(solution)/shard_map/while/body/eval_jaxpr/dot_general | solution.py:31
  297.6 4.5 %collective-permute-done.1 = f32[64,1152]{1,0:T(8,128)S(1)} collective-permute-done((f32[64,1152]{1,0:T(8,128)S(1)}, f32[64,1152]{1,0:T(8,128)S(1)}, u32[]{:S(2)}, u32[]{:S(2)}) %collective-permute-start.1) | collective-permute-done | bytes 294944 | tf_op jit(solution)/shard_map/while/body/eval_jaxpr/ppermute | solution.py:11
  304.6 5.3 %convolution_add_fusion.2 = f32[1024,1152]{1,0:T(8,128)} fusion(f32[1024,1152]{1,0:T(8,128)} %get-tuple-element.243, bf16[1024,64]{0,1:T(8,128)(2,1)S(1)} %fusion.19, bf16[64,1152]{1,0:T(8,128)(2,1)S(1)} %get-tuple-element.244), kind=kOutput, calls=%fused_computation.18 | convolution fusion | flops 152174592 | bytes 9715712 | tf_op jit(solution)/shard_map/dot_general | solution.py:31
  312.2 9.7 %collective-permute-done.2 = f32[64,1152]{1,0:T(8,128)S(1)} collective-permute-done((f32[64,1152]{1,0:T(8,128)S(1)}, f32[64,1152]{1,0:T(8,128)S(1)}, u32[]{:S(2)}, u32[]{:S(2)}) %collective-permute-start.2) | collective-permute-done | bytes 294944 | tf_op jit(solution)/shard_map/ppermute | solution.py:11
  323.0 65.8 %reduce-scatter.2.cloned.1.call-done = f32[64,1152]{1,0:T(8,128)} async-done(((f32[1024,1152]{1,0:T(8,128)}), f32[64,1152]{1,0:T(8,128)}) %reduce-scatter.2.cloned.1.call-update) | async-done | bytes 294928 | tf_op jit(solution)/shard_map/reduce_scatter | solution.py:76
  (147 shorter events, 33.1 us)
Async XLA Ops:
  7.2 77.4 %all-gather.2.cloned.1.call-start = ((), (), s32[]{:S(2)}) async-start(), calls=%async_computation.1 | async-start | bytes 2506752 | tf_op jit(solution)/shard_map/all_gather | solution.py:47
  10.1 378.8 %reduce-scatter.2.cloned.1.call-start = ((), (), s32[]{:S(2)}) async-start(), calls=%async_computation.2 | async-start | bytes 5013504 | tf_op jit(solution)/shard_map/reduce_scatter | solution.py:76
  84.6 4.1 %copy-start = (bf16[1024,1152]{1,0:T(8,128)(2,1)S(1)}, bf16[1024,1152]{1,0:T(8,128)(2,1)}, u32[]{:S(2)}) copy-start(bf16[1024,1152]{1,0:T(8,128)(2,1)} %get-tuple-element.382) | copy-start | bytes 7077892 | tf_op jit(solution)/shard_map/while
  84.7 9.1 %collective-permute-start = (bf16[64,1152]{1,0:T(8,128)(2,1)S(1)}, bf16[64,1152]{1,0:T(8,128)(2,1)S(1)}, u32[]{:S(2)}, u32[]{:S(2)}) collective-permute-start(bf16[64,1152]{1,0:T(8,128)(2,1)S(1)} %copy.11), channel_id=1, source_target_pairs={{0,16},{16,32},{32,48},{48,64},{64,80},{80,96},{96,112},{112,128},... | collective-permute-start | bytes 442376 | tf_op jit(solution)/shard_map/while/body/eval_jaxpr/ppermute | solution.py:11
  89.3 9.8 %collective-permute-start.1 = (f32[64,1152]{1,0:T(8,128)S(1)}, f32[64,1152]{1,0:T(8,128)S(1)}, u32[]{:S(2)}, u32[]{:S(2)}) collective-permute-start(f32[64,1152]{1,0:T(8,128)S(1)} %convolution_add_fusion.6), channel_id=1, source_target_pairs={{0,16},{16,32},{32,48},{48,64},{64,80},{80,96},{96,112},{112,128},... | collective-permute-start | bytes 884744 | tf_op jit(solution)/shard_map/while/body/eval_jaxpr/ppermute | solution.py:11
  99.1 4.1 %copy-start = (bf16[1024,1152]{1,0:T(8,128)(2,1)S(1)}, bf16[1024,1152]{1,0:T(8,128)(2,1)}, u32[]{:S(2)}) copy-start(bf16[1024,1152]{1,0:T(8,128)(2,1)} %get-tuple-element.382) | copy-start | bytes 7077892 | tf_op jit(solution)/shard_map/while
  99.2 10.0 %collective-permute-start = (bf16[64,1152]{1,0:T(8,128)(2,1)S(1)}, bf16[64,1152]{1,0:T(8,128)(2,1)S(1)}, u32[]{:S(2)}, u32[]{:S(2)}) collective-permute-start(bf16[64,1152]{1,0:T(8,128)(2,1)S(1)} %copy.11), channel_id=1, source_target_pairs={{0,16},{16,32},{32,48},{48,64},{64,80},{80,96},{96,112},{112,128},... | collective-permute-start | bytes 442376 | tf_op jit(solution)/shard_map/while/body/eval_jaxpr/ppermute | solution.py:11
  103.8 9.8 %collective-permute-start.1 = (f32[64,1152]{1,0:T(8,128)S(1)}, f32[64,1152]{1,0:T(8,128)S(1)}, u32[]{:S(2)}, u32[]{:S(2)}) collective-permute-start(f32[64,1152]{1,0:T(8,128)S(1)} %convolution_add_fusion.6), channel_id=1, source_target_pairs={{0,16},{16,32},{32,48},{48,64},{64,80},{80,96},{96,112},{112,128},... | collective-permute-start | bytes 884744 | tf_op jit(solution)/shard_map/while/body/eval_jaxpr/ppermute | solution.py:11
  113.6 4.1 %copy-start = (bf16[1024,1152]{1,0:T(8,128)(2,1)S(1)}, bf16[1024,1152]{1,0:T(8,128)(2,1)}, u32[]{:S(2)}) copy-start(bf16[1024,1152]{1,0:T(8,128)(2,1)} %get-tuple-element.382) | copy-start | bytes 7077892 | tf_op jit(solution)/shard_map/while
  113.6 10.0 %collective-permute-start = (bf16[64,1152]{1,0:T(8,128)(2,1)S(1)}, bf16[64,1152]{1,0:T(8,128)(2,1)S(1)}, u32[]{:S(2)}, u32[]{:S(2)}) collective-permute-start(bf16[64,1152]{1,0:T(8,128)(2,1)S(1)} %copy.11), channel_id=1, source_target_pairs={{0,16},{16,32},{32,48},{48,64},{64,80},{80,96},{96,112},{112,128},... | collective-permute-start | bytes 442376 | tf_op jit(solution)/shard_map/while/body/eval_jaxpr/ppermute | solution.py:11
  118.3 9.8 %collective-permute-start.1 = (f32[64,1152]{1,0:T(8,128)S(1)}, f32[64,1152]{1,0:T(8,128)S(1)}, u32[]{:S(2)}, u32[]{:S(2)}) collective-permute-start(f32[64,1152]{1,0:T(8,128)S(1)} %convolution_add_fusion.6), channel_id=1, source_target_pairs={{0,16},{16,32},{32,48},{48,64},{64,80},{80,96},{96,112},{112,128},... | collective-permute-start | bytes 884744 | tf_op jit(solution)/shard_map/while/body/eval_jaxpr/ppermute | solution.py:11
  128.1 4.1 %copy-start = (bf16[1024,1152]{1,0:T(8,128)(2,1)S(1)}, bf16[1024,1152]{1,0:T(8,128)(2,1)}, u32[]{:S(2)}) copy-start(bf16[1024,1152]{1,0:T(8,128)(2,1)} %get-tuple-element.382) | copy-start | bytes 7077892 | tf_op jit(solution)/shard_map/while
  128.1 10.0 %collective-permute-start = (bf16[64,1152]{1,0:T(8,128)(2,1)S(1)}, bf16[64,1152]{1,0:T(8,128)(2,1)S(1)}, u32[]{:S(2)}, u32[]{:S(2)}) collective-permute-start(bf16[64,1152]{1,0:T(8,128)(2,1)S(1)} %copy.11), channel_id=1, source_target_pairs={{0,16},{16,32},{32,48},{48,64},{64,80},{80,96},{96,112},{112,128},... | collective-permute-start | bytes 442376 | tf_op jit(solution)/shard_map/while/body/eval_jaxpr/ppermute | solution.py:11
  132.8 9.8 %collective-permute-start.1 = (f32[64,1152]{1,0:T(8,128)S(1)}, f32[64,1152]{1,0:T(8,128)S(1)}, u32[]{:S(2)}, u32[]{:S(2)}) collective-permute-start(f32[64,1152]{1,0:T(8,128)S(1)} %convolution_add_fusion.6), channel_id=1, source_target_pairs={{0,16},{16,32},{32,48},{48,64},{64,80},{80,96},{96,112},{112,128},... | collective-permute-start | bytes 884744 | tf_op jit(solution)/shard_map/while/body/eval_jaxpr/ppermute | solution.py:11
  142.6 4.1 %copy-start = (bf16[1024,1152]{1,0:T(8,128)(2,1)S(1)}, bf16[1024,1152]{1,0:T(8,128)(2,1)}, u32[]{:S(2)}) copy-start(bf16[1024,1152]{1,0:T(8,128)(2,1)} %get-tuple-element.382) | copy-start | bytes 7077892 | tf_op jit(solution)/shard_map/while
  142.6 10.0 %collective-permute-start = (bf16[64,1152]{1,0:T(8,128)(2,1)S(1)}, bf16[64,1152]{1,0:T(8,128)(2,1)S(1)}, u32[]{:S(2)}, u32[]{:S(2)}) collective-permute-start(bf16[64,1152]{1,0:T(8,128)(2,1)S(1)} %copy.11), channel_id=1, source_target_pairs={{0,16},{16,32},{32,48},{48,64},{64,80},{80,96},{96,112},{112,128},... | collective-permute-start | bytes 442376 | tf_op jit(solution)/shard_map/while/body/eval_jaxpr/ppermute | solution.py:11
  147.3 9.8 %collective-permute-start.1 = (f32[64,1152]{1,0:T(8,128)S(1)}, f32[64,1152]{1,0:T(8,128)S(1)}, u32[]{:S(2)}, u32[]{:S(2)}) collective-permute-start(f32[64,1152]{1,0:T(8,128)S(1)} %convolution_add_fusion.6), channel_id=1, source_target_pairs={{0,16},{16,32},{32,48},{48,64},{64,80},{80,96},{96,112},{112,128},... | collective-permute-start | bytes 884744 | tf_op jit(solution)/shard_map/while/body/eval_jaxpr/ppermute | solution.py:11
  157.1 4.1 %copy-start = (bf16[1024,1152]{1,0:T(8,128)(2,1)S(1)}, bf16[1024,1152]{1,0:T(8,128)(2,1)}, u32[]{:S(2)}) copy-start(bf16[1024,1152]{1,0:T(8,128)(2,1)} %get-tuple-element.382) | copy-start | bytes 7077892 | tf_op jit(solution)/shard_map/while
  157.1 10.0 %collective-permute-start = (bf16[64,1152]{1,0:T(8,128)(2,1)S(1)}, bf16[64,1152]{1,0:T(8,128)(2,1)S(1)}, u32[]{:S(2)}, u32[]{:S(2)}) collective-permute-start(bf16[64,1152]{1,0:T(8,128)(2,1)S(1)} %copy.11), channel_id=1, source_target_pairs={{0,16},{16,32},{32,48},{48,64},{64,80},{80,96},{96,112},{112,128},... | collective-permute-start | bytes 442376 | tf_op jit(solution)/shard_map/while/body/eval_jaxpr/ppermute | solution.py:11
  161.8 9.8 %collective-permute-start.1 = (f32[64,1152]{1,0:T(8,128)S(1)}, f32[64,1152]{1,0:T(8,128)S(1)}, u32[]{:S(2)}, u32[]{:S(2)}) collective-permute-start(f32[64,1152]{1,0:T(8,128)S(1)} %convolution_add_fusion.6), channel_id=1, source_target_pairs={{0,16},{16,32},{32,48},{48,64},{64,80},{80,96},{96,112},{112,128},... | collective-permute-start | bytes 884744 | tf_op jit(solution)/shard_map/while/body/eval_jaxpr/ppermute | solution.py:11
  171.6 4.1 %copy-start = (bf16[1024,1152]{1,0:T(8,128)(2,1)S(1)}, bf16[1024,1152]{1,0:T(8,128)(2,1)}, u32[]{:S(2)}) copy-start(bf16[1024,1152]{1,0:T(8,128)(2,1)} %get-tuple-element.382) | copy-start | bytes 7077892 | tf_op jit(solution)/shard_map/while
  171.6 10.0 %collective-permute-start = (bf16[64,1152]{1,0:T(8,128)(2,1)S(1)}, bf16[64,1152]{1,0:T(8,128)(2,1)S(1)}, u32[]{:S(2)}, u32[]{:S(2)}) collective-permute-start(bf16[64,1152]{1,0:T(8,128)(2,1)S(1)} %copy.11), channel_id=1, source_target_pairs={{0,16},{16,32},{32,48},{48,64},{64,80},{80,96},{96,112},{112,128},... | collective-permute-start | bytes 442376 | tf_op jit(solution)/shard_map/while/body/eval_jaxpr/ppermute | solution.py:11
  176.3 9.8 %collective-permute-start.1 = (f32[64,1152]{1,0:T(8,128)S(1)}, f32[64,1152]{1,0:T(8,128)S(1)}, u32[]{:S(2)}, u32[]{:S(2)}) collective-permute-start(f32[64,1152]{1,0:T(8,128)S(1)} %convolution_add_fusion.6), channel_id=1, source_target_pairs={{0,16},{16,32},{32,48},{48,64},{64,80},{80,96},{96,112},{112,128},... | collective-permute-start | bytes 884744 | tf_op jit(solution)/shard_map/while/body/eval_jaxpr/ppermute | solution.py:11
  186.1 4.1 %copy-start = (bf16[1024,1152]{1,0:T(8,128)(2,1)S(1)}, bf16[1024,1152]{1,0:T(8,128)(2,1)}, u32[]{:S(2)}) copy-start(bf16[1024,1152]{1,0:T(8,128)(2,1)} %get-tuple-element.382) | copy-start | bytes 7077892 | tf_op jit(solution)/shard_map/while
  186.1 10.0 %collective-permute-start = (bf16[64,1152]{1,0:T(8,128)(2,1)S(1)}, bf16[64,1152]{1,0:T(8,128)(2,1)S(1)}, u32[]{:S(2)}, u32[]{:S(2)}) collective-permute-start(bf16[64,1152]{1,0:T(8,128)(2,1)S(1)} %copy.11), channel_id=1, source_target_pairs={{0,16},{16,32},{32,48},{48,64},{64,80},{80,96},{96,112},{112,128},... | collective-permute-start | bytes 442376 | tf_op jit(solution)/shard_map/while/body/eval_jaxpr/ppermute | solution.py:11
  190.7 9.8 %collective-permute-start.1 = (f32[64,1152]{1,0:T(8,128)S(1)}, f32[64,1152]{1,0:T(8,128)S(1)}, u32[]{:S(2)}, u32[]{:S(2)}) collective-permute-start(f32[64,1152]{1,0:T(8,128)S(1)} %convolution_add_fusion.6), channel_id=1, source_target_pairs={{0,16},{16,32},{32,48},{48,64},{64,80},{80,96},{96,112},{112,128},... | collective-permute-start | bytes 884744 | tf_op jit(solution)/shard_map/while/body/eval_jaxpr/ppermute | solution.py:11
  200.6 4.1 %copy-start = (bf16[1024,1152]{1,0:T(8,128)(2,1)S(1)}, bf16[1024,1152]{1,0:T(8,128)(2,1)}, u32[]{:S(2)}) copy-start(bf16[1024,1152]{1,0:T(8,128)(2,1)} %get-tuple-element.382) | copy-start | bytes 7077892 | tf_op jit(solution)/shard_map/while
  200.6 10.0 %collective-permute-start = (bf16[64,1152]{1,0:T(8,128)(2,1)S(1)}, bf16[64,1152]{1,0:T(8,128)(2,1)S(1)}, u32[]{:S(2)}, u32[]{:S(2)}) collective-permute-start(bf16[64,1152]{1,0:T(8,128)(2,1)S(1)} %copy.11), channel_id=1, source_target_pairs={{0,16},{16,32},{32,48},{48,64},{64,80},{80,96},{96,112},{112,128},... | collective-permute-start | bytes 442376 | tf_op jit(solution)/shard_map/while/body/eval_jaxpr/ppermute | solution.py:11
  205.2 9.8 %collective-permute-start.1 = (f32[64,1152]{1,0:T(8,128)S(1)}, f32[64,1152]{1,0:T(8,128)S(1)}, u32[]{:S(2)}, u32[]{:S(2)}) collective-permute-start(f32[64,1152]{1,0:T(8,128)S(1)} %convolution_add_fusion.6), channel_id=1, source_target_pairs={{0,16},{16,32},{32,48},{48,64},{64,80},{80,96},{96,112},{112,128},... | collective-permute-start | bytes 884744 | tf_op jit(solution)/shard_map/while/body/eval_jaxpr/ppermute | solution.py:11
  215.1 4.1 %copy-start = (bf16[1024,1152]{1,0:T(8,128)(2,1)S(1)}, bf16[1024,1152]{1,0:T(8,128)(2,1)}, u32[]{:S(2)}) copy-start(bf16[1024,1152]{1,0:T(8,128)(2,1)} %get-tuple-element.382) | copy-start | bytes 7077892 | tf_op jit(solution)/shard_map/while
  215.1 10.0 %collective-permute-start = (bf16[64,1152]{1,0:T(8,128)(2,1)S(1)}, bf16[64,1152]{1,0:T(8,128)(2,1)S(1)}, u32[]{:S(2)}, u32[]{:S(2)}) collective-permute-start(bf16[64,1152]{1,0:T(8,128)(2,1)S(1)} %copy.11), channel_id=1, source_target_pairs={{0,16},{16,32},{32,48},{48,64},{64,80},{80,96},{96,112},{112,128},... | collective-permute-start | bytes 442376 | tf_op jit(solution)/shard_map/while/body/eval_jaxpr/ppermute | solution.py:11
  219.7 9.8 %collective-permute-start.1 = (f32[64,1152]{1,0:T(8,128)S(1)}, f32[64,1152]{1,0:T(8,128)S(1)}, u32[]{:S(2)}, u32[]{:S(2)}) collective-permute-start(f32[64,1152]{1,0:T(8,128)S(1)} %convolution_add_fusion.6), channel_id=1, source_target_pairs={{0,16},{16,32},{32,48},{48,64},{64,80},{80,96},{96,112},{112,128},... | collective-permute-start | bytes 884744 | tf_op jit(solution)/shard_map/while/body/eval_jaxpr/ppermute | solution.py:11
  229.6 4.1 %copy-start = (bf16[1024,1152]{1,0:T(8,128)(2,1)S(1)}, bf16[1024,1152]{1,0:T(8,128)(2,1)}, u32[]{:S(2)}) copy-start(bf16[1024,1152]{1,0:T(8,128)(2,1)} %get-tuple-element.382) | copy-start | bytes 7077892 | tf_op jit(solution)/shard_map/while
  229.6 10.0 %collective-permute-start = (bf16[64,1152]{1,0:T(8,128)(2,1)S(1)}, bf16[64,1152]{1,0:T(8,128)(2,1)S(1)}, u32[]{:S(2)}, u32[]{:S(2)}) collective-permute-start(bf16[64,1152]{1,0:T(8,128)(2,1)S(1)} %copy.11), channel_id=1, source_target_pairs={{0,16},{16,32},{32,48},{48,64},{64,80},{80,96},{96,112},{112,128},... | collective-permute-start | bytes 442376 | tf_op jit(solution)/shard_map/while/body/eval_jaxpr/ppermute | solution.py:11
  234.2 9.8 %collective-permute-start.1 = (f32[64,1152]{1,0:T(8,128)S(1)}, f32[64,1152]{1,0:T(8,128)S(1)}, u32[]{:S(2)}, u32[]{:S(2)}) collective-permute-start(f32[64,1152]{1,0:T(8,128)S(1)} %convolution_add_fusion.6), channel_id=1, source_target_pairs={{0,16},{16,32},{32,48},{48,64},{64,80},{80,96},{96,112},{112,128},... | collective-permute-start | bytes 884744 | tf_op jit(solution)/shard_map/while/body/eval_jaxpr/ppermute | solution.py:11
  244.1 4.1 %copy-start = (bf16[1024,1152]{1,0:T(8,128)(2,1)S(1)}, bf16[1024,1152]{1,0:T(8,128)(2,1)}, u32[]{:S(2)}) copy-start(bf16[1024,1152]{1,0:T(8,128)(2,1)} %get-tuple-element.382) | copy-start | bytes 7077892 | tf_op jit(solution)/shard_map/while
  244.1 10.0 %collective-permute-start = (bf16[64,1152]{1,0:T(8,128)(2,1)S(1)}, bf16[64,1152]{1,0:T(8,128)(2,1)S(1)}, u32[]{:S(2)}, u32[]{:S(2)}) collective-permute-start(bf16[64,1152]{1,0:T(8,128)(2,1)S(1)} %copy.11), channel_id=1, source_target_pairs={{0,16},{16,32},{32,48},{48,64},{64,80},{80,96},{96,112},{112,128},... | collective-permute-start | bytes 442376 | tf_op jit(solution)/shard_map/while/body/eval_jaxpr/ppermute | solution.py:11
  248.7 9.8 %collective-permute-start.1 = (f32[64,1152]{1,0:T(8,128)S(1)}, f32[64,1152]{1,0:T(8,128)S(1)}, u32[]{:S(2)}, u32[]{:S(2)}) collective-permute-start(f32[64,1152]{1,0:T(8,128)S(1)} %convolution_add_fusion.6), channel_id=1, source_target_pairs={{0,16},{16,32},{32,48},{48,64},{64,80},{80,96},{96,112},{112,128},... | collective-permute-start | bytes 884744 | tf_op jit(solution)/shard_map/while/body/eval_jaxpr/ppermute | solution.py:11
  258.6 4.1 %copy-start = (bf16[1024,1152]{1,0:T(8,128)(2,1)S(1)}, bf16[1024,1152]{1,0:T(8,128)(2,1)}, u32[]{:S(2)}) copy-start(bf16[1024,1152]{1,0:T(8,128)(2,1)} %get-tuple-element.382) | copy-start | bytes 7077892 | tf_op jit(solution)/shard_map/while
  258.6 10.0 %collective-permute-start = (bf16[64,1152]{1,0:T(8,128)(2,1)S(1)}, bf16[64,1152]{1,0:T(8,128)(2,1)S(1)}, u32[]{:S(2)}, u32[]{:S(2)}) collective-permute-start(bf16[64,1152]{1,0:T(8,128)(2,1)S(1)} %copy.11), channel_id=1, source_target_pairs={{0,16},{16,32},{32,48},{48,64},{64,80},{80,96},{96,112},{112,128},... | collective-permute-start | bytes 442376 | tf_op jit(solution)/shard_map/while/body/eval_jaxpr/ppermute | solution.py:11
  263.2 9.8 %collective-permute-start.1 = (f32[64,1152]{1,0:T(8,128)S(1)}, f32[64,1152]{1,0:T(8,128)S(1)}, u32[]{:S(2)}, u32[]{:S(2)}) collective-permute-start(f32[64,1152]{1,0:T(8,128)S(1)} %convolution_add_fusion.6), channel_id=1, source_target_pairs={{0,16},{16,32},{32,48},{48,64},{64,80},{80,96},{96,112},{112,128},... | collective-permute-start | bytes 884744 | tf_op jit(solution)/shard_map/while/body/eval_jaxpr/ppermute | solution.py:11
  273.1 10.0 %collective-permute-start = (bf16[64,1152]{1,0:T(8,128)(2,1)S(1)}, bf16[64,1152]{1,0:T(8,128)(2,1)S(1)}, u32[]{:S(2)}, u32[]{:S(2)}) collective-permute-start(bf16[64,1152]{1,0:T(8,128)(2,1)S(1)} %copy.11), channel_id=1, source_target_pairs={{0,16},{16,32},{32,48},{48,64},{64,80},{80,96},{96,112},{112,128},... | collective-permute-start | bytes 442376 | tf_op jit(solution)/shard_map/while/body/eval_jaxpr/ppermute | solution.py:11
  277.7 9.8 %collective-permute-start.1 = (f32[64,1152]{1,0:T(8,128)S(1)}, f32[64,1152]{1,0:T(8,128)S(1)}, u32[]{:S(2)}, u32[]{:S(2)}) collective-permute-start(f32[64,1152]{1,0:T(8,128)S(1)} %convolution_add_fusion.6), channel_id=1, source_target_pairs={{0,16},{16,32},{32,48},{48,64},{64,80},{80,96},{96,112},{112,128},... | collective-permute-start | bytes 884744 | tf_op jit(solution)/shard_map/while/body/eval_jaxpr/ppermute | solution.py:11
  287.6 10.0 %collective-permute-start = (bf16[64,1152]{1,0:T(8,128)(2,1)S(1)}, bf16[64,1152]{1,0:T(8,128)(2,1)S(1)}, u32[]{:S(2)}, u32[]{:S(2)}) collective-permute-start(bf16[64,1152]{1,0:T(8,128)(2,1)S(1)} %copy.11), channel_id=1, source_target_pairs={{0,16},{16,32},{32,48},{48,64},{64,80},{80,96},{96,112},{112,128},... | collective-permute-start | bytes 442376 | tf_op jit(solution)/shard_map/while/body/eval_jaxpr/ppermute | solution.py:11
  292.2 9.8 %collective-permute-start.1 = (f32[64,1152]{1,0:T(8,128)S(1)}, f32[64,1152]{1,0:T(8,128)S(1)}, u32[]{:S(2)}, u32[]{:S(2)}) collective-permute-start(f32[64,1152]{1,0:T(8,128)S(1)} %convolution_add_fusion.6), channel_id=1, source_target_pairs={{0,16},{16,32},{32,48},{48,64},{64,80},{80,96},{96,112},{112,128},... | collective-permute-start | bytes 884744 | tf_op jit(solution)/shard_map/while/body/eval_jaxpr/ppermute | solution.py:11
  309.9 12.0 %copy-start.2 = (f32[64,1152]{1,0:T(8,128)S(1)}, f32[64,1152]{1,0:T(8,128)}, u32[]{:S(2)}) copy-start(f32[64,1152]{1,0:T(8,128)} %param.7) | copy-start | bytes 884740
  309.9 78.9 %copy-start.3 = (f32[64,1152]{1,0:T(8,128)S(1)}, f32[64,1152]{1,0:T(8,128)}, u32[]{:S(2)}) copy-start(f32[64,1152]{1,0:T(8,128)} %param.6) | copy-start | bytes 884740
  312.1 9.8 %collective-permute-start.2 = (f32[64,1152]{1,0:T(8,128)S(1)}, f32[64,1152]{1,0:T(8,128)S(1)}, u32[]{:S(2)}, u32[]{:S(2)}) collective-permute-start(f32[64,1152]{1,0:T(8,128)S(1)} %convolution_add_fusion.3), channel_id=1, source_target_pairs={{0,16},{16,32},{32,48},{48,64},{64,80},{80,96},{96,112},{112,128},... | collective-permute-start | bytes 884744 | tf_op jit(solution)/shard_map/ppermute | solution.py:11
  (3 other events, 9.9 us)
Sparse Core Ops, SparseCore 0:
  10.4 74.1 all-gather.1
  310.0 78.7 reduce-scatter.1
where the time goes:
time: 400 us; the launch traced here: 399 us
  waiting for transfers between devices  215 us (54%)
  matrix products  153 us (38%)
  between operations  15.4 us (4%)
  other arithmetic  9.04 us (2%)
  starting transfers between devices  4.07 us (1%)
    dot_general x16, matrix products, tile_terms(): image_part = jnp.dot(coef, text_tile, preferred_element_type=jnp.float32)  82.2 us
    ppermute x31, waiting for transfers between devices, from_behind(): return lax.ppermute(x, axis, [(i, (i + by) % peers) for i in range(peers)])  77.6 us
    all_gather x1, waiting for transfers between devices, body(): group_images = lax.all_gather(image_hat, 'row', axis=0, tiled=True)  71 us
    reduce_scatter x1, waiting for transfers between devices, body(): lax.psum_scatter(image_acc, 'row', scatter_dimension=0, tiled=True)  65.8 us
    dot_general x16, matrix products, tile_terms(): jnp.einsum('id,jd->ij', group_images, text_tile, preferred_element_type=j...  62.1 us
    dot_general x16, matrix products, tile_terms(): jnp.einsum('ij,id->jd', coef, group_images, preferred_element_type=jnp.fl...  8.53 us
  transfers between devices with their start and end apart: 33, of which 18 were waited for; matrix products, arithmetic and copies ran while one was open for 37% of the time, Pallas kernels for 0%

commit v1 on v0

v1 whole, which is shorter than its diff:
```python
import jax
import jax.numpy as jnp
from jax import lax
from jax.experimental import pallas as pl
from jax.experimental.pallas import tpu as pltpu
from jax.sharding import PartitionSpec as P

EPS = 1e-06
F32 = jnp.float32
BF16 = jnp.bfloat16
MESH = pl.DeviceIdType.MESH
NT = (((1,), (1,)), ((), ()))
NN = (((1,), (0,)), ((), ()))
TN = (((0,), (0,)), ((), ()))

NX, NY, NZ = 4, 4, 8
ROWS = 64
HALF = 32
QUAR = 16
XP, XM = (1, 0, 0, 0), (-1, 0, 0, 0)
YP, YM = (0, 1, 0, 0), (0, -1, 0, 0)
ZP, ZM = (0, 0, 1, 0), (0, 0, -1, 0)
CORE = (0, 0, 0, 1)
NEIGHBOURS = (XP, XM, YP, YM, ZP, ZM, CORE)

IMAGE_ORDER = (
    (2, 2), (2, 1), (2, 3), (1, 2),
    (3, 2), (2, 0), (0, 2), (1, 1),
    (1, 3), (3, 1), (3, 3), (0, 1),
    (0, 3), (1, 0), (3, 0), (0, 0),
)
IMAGE_ROW = {slot: i * ROWS for i, slot in enumerate(IMAGE_ORDER)}
TEXT_ORDER = (4, 3, 5, 2, 6, 1, 7, 0)
TEXT_ROW = {(dz, dc): (i * 2 + dc) * ROWS for i, dz in enumerate(TEXT_ORDER) for dc in range(2)}
NI = len(IMAGE_ORDER) * ROWS
NTX = len(TEXT_ORDER) * 2 * ROWS
BLOCK = 256
MESSAGES = 160


def position():
    blk = lax.axis_index("blk")
    row = lax.axis_index("row")
    return (blk // 2) % NX, (blk // (2 * NX)) * 2 + row // NZ, row % NZ, blk % 2


def device(here, step):
    x = (here[0] + step[0] + NX) % NX
    y = (here[1] + step[1] + NY) % NY
    z = (here[2] + step[2] + NZ) % NZ
    core = (here[3] + step[3]) % 2
    return (((y // 2) * NX + x) * 2 + core, (y % 2) * NZ + z)


def unit_of(values):
    norm_rows = jnp.sqrt(jnp.sum(values * values, axis=1, keepdims=True) + EPS)
    return values / norm_rows, norm_rows


def project_back(grad_hat, unit_rows, norm_rows):
    return (grad_hat - unit_rows * jnp.sum(unit_rows * grad_hat, axis=1, keepdims=True)) / norm_rows


def kernel(
    images, texts, scale, bias, image_grad, text_grad,
    image_hat, text_hat, image_acc, text_acc, coef, out_stage, in_stage, send_sem, recv_sem,
):
    here = position()
    barrier = pltpu.get_barrier_semaphore()
    for step in NEIGHBOURS:
        pl.semaphore_signal(barrier, inc=1, device_id=device(here, step), device_id_type=MESH)
    scale_value = scale[0]
    bias_value = bias[0]

    own_image = pl.ds(IMAGE_ROW[0, 0], ROWS)
    own_text = pl.ds(TEXT_ROW[0, 0], ROWS)
    image_hat[own_image] = unit_of(images[...])[0].astype(BF16)
    text_hat[own_text] = unit_of(texts[...])[0].astype(BF16)
    pl.semaphore_wait(barrier, len(NEIGHBOURS))

    copies = []
    staged = [0]

    def send(src, dst, step):
        n = len(copies)
        assert n < MESSAGES
        copy = pltpu.make_async_remote_copy(
            src_ref=src, dst_ref=dst, send_sem=send_sem.at[n], recv_sem=recv_sem.at[n],
            device_id=device(here, step), device_id_type=MESH,
        )
        copy.start()
        copies.append(copy)
        return copy

    def wait(*arriving):
        for copy in arriving:
            copy.wait_recv()

    def pass_image(step, slot, start, count):
        to = ((slot[0] - step[0]) % NX, (slot[1] - step[1]) % NY)
        return send(
            image_hat.at[pl.ds(IMAGE_ROW[slot] + start, count)],
            image_hat.at[pl.ds(IMAGE_ROW[to] + start, count)],
            step,
        )

    def pass_text(step, dz, start, count):
        to = ((dz - step[2]) % NZ, step[3])
        return send(
            text_hat.at[pl.ds(TEXT_ROW[dz, 0] + start, count)],
            text_hat.at[pl.ds(TEXT_ROW[to] + start, count)],
            step,
        )

    def both(first, second, slot, start):
        return (pass_image(first, slot, start, HALF), pass_image(second, slot, start, HALF))

    def onward_y(dx, start):
        return (pass_image(YP, (dx, 3), start, QUAR), pass_image(YM, (dx, 1), start + QUAR, QUAR))

    def onward_x(dy, start):
        return (pass_image(XP, (3, dy), start, QUAR), pass_image(XM, (1, dy), start + QUAR, QUAR))

    h1, h2 = 0, HALF
    x1 = both(XP, XM, (0, 0), h1)
    y2 = both(YP, YM, (0, 0), h2)
    za = (pass_text(ZP, 0, 0, HALF), pass_text(ZM, 0, 0, HALF))
    x2 = both(XP, XM, (0, 0), h2)
    y1 = both(YP, YM, (0, 0), h1)
    zb = (pass_text(ZP, 0, HALF, HALF), pass_text(ZM, 0, HALF, HALF))
    last = [pass_text(CORE, 0, 0, ROWS)]

    wait(*x1)
    xf1 = onward_x(0, h1)
    y1_3 = both(YP, YM, (3, 0), h1)
    y1_1 = both(YP, YM, (1, 0), h1)
    wait(*y2)
    yf2 = onward_y(0, h2)
    x2_3 = both(XP, XM, (0, 3), h2)
    x2_1 = both(XP, XM, (0, 1), h2)
    wait(*za)
    za = (pass_text(ZP, 7, 0, HALF), pass_text(ZM, 1, 0, HALF))
    wait(*y1)
    last += onward_y(0, h1)
    wait(*x2)
    last += onward_x(0, h2)
    wait(*zb)
    zb = (pass_text(ZP, 7, HALF, HALF), pass_text(ZM, 1, HALF, HALF))
    last += [pass_text(CORE, 7, 0, ROWS), pass_text(CORE, 1, 0, ROWS)]
    wait(*xf1)
    y1_2 = both(YP, YM, (2, 0), h1)
    wait(*yf2)
    x2_2 = both(XP, XM, (0, 2), h2)
    wait(*za)
    za = (pass_text(ZP, 6, 0, HALF), pass_text(ZM, 2, 0, HALF))
    wait(*y1_3)
    last += onward_y(3, h1)
    wait(*x2_3)
    last += onward_x(3, h2)
    wait(*zb)
    zb = (pass_text(ZP, 6, HALF, HALF), pass_text(ZM, 2, HALF, HALF))
    last += [pass_text(CORE, 6, 0, ROWS), pass_text(CORE, 2, 0, ROWS)]
    wait(*y1_1)
    last += onward_y(1, h1)
    wait(*x2_1)
    last += onward_x(1, h2)
    wait(*za)
    z4 = [pass_text(ZP, 5, 0, HALF)]
    wait(*zb)
    z4 += [pass_text(ZM, 3, HALF, HALF)]
    last += [pass_text(CORE, 5, 0, ROWS), pass_text(CORE, 3, 0, ROWS)]
    wait(*y1_2)
    last += onward_y(2, h1)
    wait(*x2_2)
    last += onward_x(2, h2)
    wait(*z4)
    last += [pass_text(CORE, 4, 0, ROWS)]
    wait(*last)

    for block in range(NI // BLOCK):
        rows = pl.ds(block * BLOCK, BLOCK)
        logits = scale_value * lax.dot_general(image_hat[rows], text_hat[...], NT, preferred_element_type=F32) + bias_value
        coef[rows] = (scale_value * jax.nn.sigmoid(logits)).astype(BF16)
        if block * BLOCK <= IMAGE_ROW[0, 0] < (block + 1) * BLOCK:
            top = IMAGE_ROW[0, 0] - block * BLOCK
            left = TEXT_ROW[0, 0]
            pair = logits[top : top + ROWS, left : left + 2 * ROWS]
            sign = jnp.where(
                lax.broadcasted_iota(jnp.int32, pair.shape, 0) == lax.broadcasted_iota(jnp.int32, pair.shape, 1), 1.0, -1.0
            ).astype(F32)
            coef[own_image, pl.ds(left, 2 * ROWS)] = (-scale_value * sign * jax.nn.sigmoid(-sign * pair)).astype(BF16)

    def image_block(block):
        rows = pl.ds(block * BLOCK, BLOCK)
        image_acc[rows] = lax.dot_general(coef[rows], text_hat[...], NN, preferred_element_type=F32)

    def text_block(start, count):
        rows = pl.ds(start, count)
        text_acc[rows] = lax.dot_general(coef[:, rows], image_hat[...], TN, preferred_element_type=F32)

    def ship(acc, row, to_row, count, step):
        at = staged[0]
        staged[0] += count
        piece = pl.ds(at, count)
        out_stage[piece] = acc[pl.ds(row, count)].astype(BF16)
        return (send(out_stage.at[piece], in_stage.at[piece], step), acc, to_row, count, at)

    def absorb(*messages):
        for copy, acc, row, count, at in messages:
            copy.wait_recv()
            rows = pl.ds(row, count)
            acc[rows] = acc[rows] + in_stage[pl.ds(at, count)].astype(F32)

    def ship_image(step, slot, start, count):
        to = ((slot[0] - step[0]) % NX, (slot[1] - step[1]) % NY)
        return ship(image_acc, IMAGE_ROW[slot] + start, IMAGE_ROW[to] + start, count, step)

    def ship_text(step, dz, start, count):
        to = ((dz - step[2]) % NZ, 0)
        return ship(text_acc, TEXT_ROW[dz, step[3]] + start, TEXT_ROW[to] + start, count, step)

    def far_y(dx, start):
        return (ship_image(YM, (dx, 2), start, QUAR), ship_image(YP, (dx, 2), start + QUAR, QUAR))

    def near_y(dx, start):
        return (ship_image(YM, (dx, 3), start, HALF), ship_image(YP, (dx, 1), start, HALF))

    def far_x(dy, start):
        return (ship_image(XM, (2, dy), start, QUAR), ship_image(XP, (2, dy), start + QUAR, QUAR))

    def near_x(dy, start):
        return (ship_image(XM, (3, dy), start, HALF), ship_image(XP, (1, dy), start, HALF))

    fy, fx, ny, nx = {}, {}, {}, {}
    text_block(0, 512)
    c4, c3, c5, c2 = [ship_text(CORE, dz, 0, ROWS) for dz in (4, 3, 5, 2)]
    image_block(0)
    fy[2], fx[2] = far_y(2, h1), far_x(2, h2)
    fy[1], fx[1] = far_y(1, h1), far_x(1, h2)
    fx[3] = far_x(3, h2)
    absorb(c4, c3, c5)
    za, zb = ship_text(ZP, 4, 0, HALF), ship_text(ZM, 4, HALF, HALF)
    zc, zd = ship_text(ZP, 3, HALF, HALF), ship_text(ZM, 5, 0, HALF)
    image_block(1)
    fy[3], fy[0] = far_y(3, h1), far_y(0, h1)
    fx[0] = far_x(0, h2)
    text_block(512, 512)
    c6, c1, c7, c0 = [ship_text(CORE, dz, 0, ROWS) for dz in (6, 1, 7, 0)]
    absorb(*fy[2])
    ny[2] = near_y(2, h1)
    absorb(*fx[2])
    nx[2] = near_x(2, h2)
    image_block(2)
    absorb(za, zb)
    za, zb = ship_text(ZP, 3, 0, HALF), ship_text(ZM, 5, HALF, HALF)
    absorb(*fx[1])
    nx[1] = near_x(1, h2)
    absorb(*fy[1])
    ny[1] = near_y(1, h1)
    image_block(3)
    absorb(*fx[3])
    nx[3] = near_x(3, h2)
    absorb(*fy[3])
    ny[3] = near_y(3, h1)
    absorb(c2, c6)
    absorb(zc, zd)
    zc, zd = ship_text(ZP, 2, HALF, HALF), ship_text(ZM, 6, 0, HALF)
    absorb(*fy[0])
    ny[0] = near_y(0, h1)
    absorb(*fx[0])
    nx[0] = near_x(0, h2)
    absorb(za, zb)
    za, zb = ship_text(ZP, 2, 0, HALF), ship_text(ZM, 6, HALF, HALF)
    absorb(*ny[2])
    gx = far_x(0, h1)
    absorb(*nx[2])
    gy = far_y(0, h2)
    absorb(c1, c7)
    absorb(zc, zd)
    zc, zd = ship_text(ZP, 1, HALF, HALF), ship_text(ZM, 7, 0, HALF)
    absorb(*ny[1], *ny[3])
    absorb(*nx[1], *nx[3])
    absorb(*gx)
    kx = near_x(0, h1)
    absorb(*gy)
    ky = near_y(0, h2)
    absorb(za, zb)
    za, zb = ship_text(ZP, 1, 0, HALF), ship_text(ZM, 7, HALF, HALF)
    absorb(c0)
    absorb(*ny[0])
    absorb(*nx[0])
    absorb(*kx, *ky)
    image_unit, image_norm = unit_of(images[...])
    image_grad[...] = project_back(image_acc[own_image], image_unit, image_norm)
    absorb(zc, zd, za, zb)
    text_unit, text_norm = unit_of(texts[...])
    text_grad[...] = project_back(text_acc[own_text], text_unit, text_norm)
    for copy in copies:
        copy.wait_send()


def body(images, texts, scale, bias):
    width = images.shape[1]
    vmem = pl.BlockSpec(memory_space=pltpu.VMEM)
    smem = pl.BlockSpec(memory_space=pltpu.SMEM)
    shard = jax.ShapeDtypeStruct(images.shape, F32)
    return pl.pallas_call(
        kernel,
        out_shape=(shard, shard),
        in_specs=[vmem, vmem, smem, smem],
        out_specs=(vmem, vmem),
        scratch_shapes=[
            pltpu.VMEM((NI, width), BF16),
            pltpu.VMEM((NTX, width), BF16),
            pltpu.VMEM((NI, width), F32),
            pltpu.VMEM((NTX, width), F32),
            pltpu.VMEM((NI, NTX), BF16),
            pltpu.VMEM((2048, width), BF16),
            pltpu.VMEM((2048, width), BF16),
            pltpu.SemaphoreType.DMA((MESSAGES,)),
            pltpu.SemaphoreType.DMA((MESSAGES,)),
        ],
        compiler_params=pltpu.CompilerParams(
            collective_id=0, has_side_effects=True, vmem_limit_bytes=48 * 2**20
        ),
    )(images, texts, scale, bias)


def solution(mesh):
    placed = (P(("blk", "row"), None), P(("blk", "row"), None), P(), P())
    return jax.shard_map(
        body,
        mesh=mesh,
        in_specs=placed,
        out_specs=(P(("blk", "row"), None), P(("blk", "row"), None)),
        check_vma=False,
    )
```

time: 400 us -> 60.4 us (0.15)
  the two profiles are of different devices: /device:TPU:8 before, /device:TPU:1 now
where the time goes in v1:
time: 60.4 us; the launch traced here: 60.2 us
  Pallas kernels  55 us (91%)
  local copies, waits for them, and re-layouts  3.35 us (6%)
  between operations  1.94 us (3%)
    pallas_call x1, Pallas kernels, body(): pl.pallas_call(kernel, out_shape=(shard, shard), in_specs=[vmem, vmem, sm...  55 us
    unnamed x6, local copies, waits for them, and re-layouts  3.35 us

profile of v1, /device:TPU:1, one launch (start us, length us, event | category | flops | bytes accessed | tf_op | source)
XLA Modules:
  0.0 60.2 jit_solution(13013022946140092102)
XLA Ops:
  1.9 0.0 copy-start
  1.9 1.0 %copy-done = f32[64,1152]{1,0:T(8,128)S(1)} copy-done((f32[64,1152]{1,0:T(8,128)S(1)}, f32[64,1152]{1,0:T(8,128)}, u32[]{:S(2)}) %copy-start) | copy-done | bytes 294936
  2.9 0.0 copy-start.1
  2.9 1.0 %copy-done.1 = f32[64,1152]{1,0:T(8,128)S(1)} copy-done((f32[64,1152]{1,0:T(8,128)S(1)}, f32[64,1152]{1,0:T(8,128)}, u32[]{:S(2)}) %copy-start.1) | copy-done | bytes 294936
  3.8 55.0 %shard_map.59 = (f32[64,1152]{1,0:T(8,128)S(1)}, f32[64,1152]{1,0:T(8,128)S(1)}) custom-call(f32[64,1152]{1,0:T(8,128)S(1)} %copy-done, f32[64,1152]{1,0:T(8,128)S(1)} %copy-done.1, f32[1]{0:T(128)S(6)} %copy.8.scale, f32[1]{0:T(128)S(6)} %copy.9.bias), custom_call_target="tpu_custom_call" | custom-call | tf_op jit(solution)/shard_map/pallas_call | solution.py:307
  58.8 0.7 %copy.10 = f32[64,1152]{1,0:T(8,128)} copy(f32[64,1152]{1,0:T(8,128)S(1)} %get-tuple-element.4) | data formatting | bytes 589824
  59.5 0.7 %copy.11 = f32[64,1152]{1,0:T(8,128)} copy(f32[64,1152]{1,0:T(8,128)S(1)} %get-tuple-element.5) | data formatting | bytes 589824
Async XLA Ops:
  1.9 1.0 %copy-start = (f32[64,1152]{1,0:T(8,128)S(1)}, f32[64,1152]{1,0:T(8,128)}, u32[]{:S(2)}) copy-start(f32[64,1152]{1,0:T(8,128)} %images.1) | copy-start | bytes 884740
  2.9 1.0 %copy-start.1 = (f32[64,1152]{1,0:T(8,128)S(1)}, f32[64,1152]{1,0:T(8,128)}, u32[]{:S(2)}) copy-start(f32[64,1152]{1,0:T(8,128)} %texts.1) | copy-start | bytes 884740

commit v2 on v0

v2 whole, which is shorter than its diff:
```python
import jax
import jax.numpy as jnp
from jax import lax
from jax.experimental import pallas as pl
from jax.experimental.pallas import tpu as pltpu
from jax.sharding import PartitionSpec as P

EPS = 1e-06
F32 = jnp.float32
BF16 = jnp.bfloat16
MESH = pl.DeviceIdType.MESH
NT = (((1,), (1,)), ((), ()))
NN = (((1,), (0,)), ((), ()))
TN = (((0,), (0,)), ((), ()))

NX, NY, NZ = 4, 4, 8
ROWS = 64
HALF = 32
QUAR = 16
BLOCK = 256
LANES = 128
XP, XM = (1, 0, 0, 0), (-1, 0, 0, 0)
YP, YM = (0, 1, 0, 0), (0, -1, 0, 0)
ZP, ZM, ZP2, ZM2 = (0, 0, 1, 0), (0, 0, -1, 0), (0, 0, 2, 0), (0, 0, -2, 0)
CORE = (0, 0, 0, 1)
PARTNERS = (XP, XM, YP, YM, ZP, ZM, ZP2, ZM2, CORE)

IMAGE_ORDER = (
    (2, 2), (1, 2), (3, 2), (2, 1),
    (2, 3), (2, 0), (0, 2), (1, 1),
    (3, 1), (1, 3), (3, 3), (0, 1),
    (0, 3), (1, 0), (3, 0), (0, 0),
)
IMAGE_ROW = {slot: i * ROWS for i, slot in enumerate(IMAGE_ORDER)}
TEXT_ORDER = (4, 3, 5, 2, 6, 1, 7, 0)
NI = len(IMAGE_ORDER) * ROWS
NTH = len(TEXT_ORDER) * ROWS
NTX = 2 * NTH
TEXT_ROW = {(dz, dc): dc * NTH + i * ROWS for i, dz in enumerate(TEXT_ORDER) for dc in range(2)}
OWN_HI, OWN_LO, OTHER_HI, OTHER_LO = 0, BLOCK, NTH, NTH + BLOCK
OWN_IMAGE, OWN_TEXT = IMAGE_ROW[0, 0], TEXT_ROW[0, 0]
STAGE = 2176
GROUPS = 64
(
    X1, X2, Y1, Y2, XD, YD, Y1_1, Y1_2, Y1_3, X2_1, X2_2, X2_3, LY0, LY1, LY2, LY3, LX0, LX1, LX2,
    LX3, ZA0, ZA1, ZA2, ZB0, ZB1, ZB2, ZC, ZD, T0, T1, T2, T3, T4, COH0, COH1, COH2, COH3, COL0, COL1,
    COL2, COL3, CPH0, CPH1, CPH2, CPH3, CPL0, CPL1, CPL2, CPL3, I0, I1, I2, I3, OH, OL, PH, PL, S0,
    S1, FX0, FX1, FX2, FX3, FY0, FY1, FY2, FY3, NX0, NX1, NX2, NX3, NY0, NY1, NY2, NY3, GX, GY, KX,
    KY, RA1, RA2, RA3, RB1, RB2, RB3, RC, RD, END_IMAGE, END_TEXT, LA, LB, Z4,
) = range(92)
Y1S, X2S = (Y1, Y1_1, Y1_2, Y1_3), (X2, X2_1, X2_2, X2_3)
LX, LY, I = (LX0, LX1, LX2, LX3), (LY0, LY1, LY2, LY3), (I0, I1, I2, I3)
FX, FY, NX_, NY_ = (FX0, FX1, FX2, FX3), (FY0, FY1, FY2, FY3), (NX0, NX1, NX2, NX3), (NY0, NY1, NY2, NY3)
COH, COL = (COH0, COH1, COH2, COH3), (COL0, COL1, COL2, COL3)
CPH, CPL = (CPH0, CPH1, CPH2, CPH3), (CPL0, CPL1, CPL2, CPL3)

ORDER = (
    ZA0, X1, Y2, ZB0, X2, Y1, Y1_1, ZA1, XD, X2_3, T0, YD, X2_1, Y1_3, ZB1, ZA2, T1, Y1_2, X2_2, T2, ZB2,
    LY0, COL3, ZD, LX0, ZC, LX3, LY3, LY1, COL2, LX1, CPL3, LX2, LY2, T3, COL1, CPL2, CPL1, T4, COH2,
    CPH0, CPH2, COL0, CPH3, CPH1, CPL0, COH0, I0, COH3, PH, S0, FY3, FX2, FY2, COH1, I1, OH, RD, RC, FY1,
    FX1, FX3, NX2, RB3, NY2, FY0, I2, PL, S1, FX0, NY1, RA3, NX1, OL, NY3, RB2, GX, NX3, GY, RA2, I3, NX0,
    NY0, RB1, KX, KY, RA1, END_IMAGE, END_TEXT,
)


class Plan:
    def __init__(self, run):
        self.run = run
        self.parts = {}
        self.coming = {}
        self.taken = set()
        self.staged = NTH
        self.steps = {}
        self.gather()
        self.compute()
        self.reduce()

    def add(self, name, after, needs, *actions):
        self.steps[name] = (after, needs, actions)

    def execute(self, order):
        done = set()
        for name in order:
            after, needs, actions = self.steps[name]
            assert done.issuperset(needs)
            self.take(after)
            for action, *args in actions:
                action(*args)
            done.add(name)

    def take(self, names):
        for name in names:
            if name not in self.taken:
                self.taken.add(name)
                self.run.wait(name)
                for key, start, count, at in self.coming.get(name, ()):
                    self.parts.setdefault(key, []).append((start, count, at))

    def pass_image(self, name, step, slot, start, count):
        to = ((slot[0] - step[0]) % NX, (slot[1] - step[1]) % NY)
        self.run.copy(name, 0, "image", IMAGE_ROW[slot] + start, "image", IMAGE_ROW[to] + start, count, step)

    def pass_text(self, name, step, dz, start, count):
        to = (dz - step[2]) % NZ
        self.run.copy(name, 0, "text", TEXT_ROW[dz, 0] + start, "text", TEXT_ROW[to, 0] + start, count, step)

    def share(self, name, dz, slots):
        self.run.copy(name, 0, "text", TEXT_ROW[dz, 0], "text", TEXT_ROW[dz, 1], slots * ROWS, CORE)

    def both_x(self, name, dy, start):
        self.pass_image(name, XP, (0, dy), start, HALF)
        self.pass_image(name, XM, (0, dy), start, HALF)

    def both_y(self, name, dx, start):
        self.pass_image(name, YP, (dx, 0), start, HALF)
        self.pass_image(name, YM, (dx, 0), start, HALF)

    def onward_x(self, name, dy, start):
        self.pass_image(name, XP, (3, dy), start, QUAR)
        self.pass_image(name, XM, (1, dy), start + QUAR, QUAR)

    def onward_y(self, name, dx, start):
        self.pass_image(name, YP, (dx, 3), start, QUAR)
        self.pass_image(name, YM, (dx, 1), start + QUAR, QUAR)

    def ring(self, name, up, down, start):
        self.pass_text(name, ZP, up, start, HALF)
        self.pass_text(name, ZM, down, start, HALF)

    def gather(self):
        add, h1, h2 = self.add, 0, HALF
        add(X1, (), (), (self.both_x, X1, 0, h1))
        add(X2, (), (), (self.both_x, X2, 0, h2))
        add(Y1, (), (), (self.both_y, Y1, 0, h1))
        add(Y2, (), (), (self.both_y, Y2, 0, h2))
        add(XD, (X1,), (), (self.onward_x, XD, 0, h1))
        add(YD, (Y2,), (), (self.onward_y, YD, 0, h2))
        for d, far, near in ((3, X1, Y2), (1, X1, Y2), (2, XD, YD)):
            add(Y1S[d], (far,), (), (self.both_y, Y1S[d], d, h1))
            add(X2S[d], (near,), (), (self.both_x, X2S[d], d, h2))
        for d, group in enumerate((LA, LB, LB, LA)):
            add(LY[d], (Y1S[d],), (), (self.onward_y, group, d, h1))
            add(LX[d], (X2S[d],), (), (self.onward_x, group, d, h2))
        add(ZA0, (), (), (self.ring, ZA0, 0, 0, 0))
        add(ZB0, (), (), (self.ring, ZB0, 0, 0, HALF))
        add(ZA1, (ZA0,), (), (self.ring, ZA1, 7, 1, 0))
        add(ZB1, (ZB0,), (), (self.ring, ZB1, 7, 1, HALF))
        add(ZA2, (ZA1,), (), (self.ring, ZA2, 6, 2, 0))
        add(ZB2, (ZB1,), (), (self.ring, ZB2, 6, 2, HALF))
        add(ZC, (ZA1,), (), (self.pass_text, Z4, ZP2, 6, 0, HALF))
        add(ZD, (ZB1,), (), (self.pass_text, Z4, ZM2, 2, HALF, HALF))
        add(T0, (), (), (self.share, T0, 0, 1))
        add(T1, (ZA0, ZB0), (), (self.share, T1, 1, 2))
        add(T2, (ZA1, ZB1), (), (self.share, T2, 2, 2))
        add(T3, (ZA2, ZB2), (), (self.share, T3, 3, 2))
        add(T4, (Z4,), (ZC, ZD), (self.share, T4, 4, 1))

    def compute(self):
        run = self.run
        images = (
            (LA, LB, X2_2, Y1_2),
            (Y1_2, XD, YD, LA, Y1_1, X2_1),
            (Y1_3, Y1_1, X2_1, X2_3, Y1, Y2),
            (X1, X2, Y1, Y2),
        )
        texts = (
            (OH, COH, OWN_HI, (ZA1, ZB1, ZA2, ZB2, Z4)),
            (OL, COL, OWN_LO, (ZA0, ZB0, ZA1, ZB1)),
            (PH, CPH, OTHER_HI, (T2, T3, T4)),
            (PL, CPL, OTHER_LO, (T0, T1, T2)),
        )
        sent = {LA: (LY0, LX0, LY3, LX3), LB: (LY1, LX1, LY2, LX2), Z4: (ZC, ZD)}
        for block, here in enumerate(images):
            for _, coefs, start, there in texts:
                waits = here + there
                needs = sum((sent.get(wait, (wait,)) for wait in waits), ())
                self.add(coefs[block], waits, needs, (run.coef, block, start))
        for block in range(4):
            self.add(I[block], (), (COH[block], COL[block], CPH[block], CPL[block]), (run.images, block))
        for name, coefs, start, _ in texts:
            self.add(name, (), coefs, (run.texts, start))

    def ship(self, name, key, to_key, start, count, step):
        at = self.staged
        self.staged += count
        self.run.stage(key[0], self.row(key), self.parts.get(key, ()), start, count, at)
        self.run.copy(name, 1, "out", at, "in", at, count, step)
        self.coming.setdefault(name, []).append((to_key, start, count, at))

    def row(self, key):
        return IMAGE_ROW[key[1]] if key[0] == "image" else TEXT_ROW[key[1]]

    def ship_image(self, name, step, slot, start, count):
        to = ((slot[0] - step[0]) % NX, (slot[1] - step[1]) % NY)
        self.ship(name, ("image", slot), ("image", to), start, count, step)

    def ship_text(self, name, step, dz, start, count):
        self.ship(name, ("text", (dz, 0)), ("text", ((dz - step[2]) % NZ, 0)), start, count, step)

    def swap(self, name, first, slots):
        start, count = TEXT_ROW[first, 1], slots * ROWS
        at = start - NTH
        self.run.stage("text", start, (), 0, count, at)
        self.run.copy(name, 1, "out", at, "in", at, count, CORE)
        self.coming[name] = [
            (("text", (dz, 0)), 0, ROWS, TEXT_ROW[dz, 0]) for dz in TEXT_ORDER if at <= TEXT_ROW[dz, 0] < at + count
        ]

    def far_x(self, name, dy, start):
        self.ship_image(name, XM, (2, dy), start, QUAR)
        self.ship_image(name, XP, (2, dy), start + QUAR, QUAR)

    def far_y(self, name, dx, start):
        self.ship_image(name, YM, (dx, 2), start, QUAR)
        self.ship_image(name, YP, (dx, 2), start + QUAR, QUAR)

    def near_x(self, name, dy, start):
        self.ship_image(name, XM, (3, dy), start, HALF)
        self.ship_image(name, XP, (1, dy), start, HALF)

    def near_y(self, name, dx, start):
        self.ship_image(name, YM, (dx, 3), start, HALF)
        self.ship_image(name, YP, (dx, 1), start, HALF)

    def ring_back(self, name, up, down, start):
        self.ship_text(name, ZP, up, start, HALF)
        self.ship_text(name, ZM, down, start, HALF)

    def reduce(self):
        add, run, h1, h2 = self.add, self.run, 0, HALF

        def blocks(*slots):
            return tuple(sorted({I[IMAGE_ROW[slot] // BLOCK] for slot in slots}))

        for d in range(4):
            add(FY[d], (), blocks((d, 2)), (self.far_y, FY[d], d, h1))
            add(FX[d], (), blocks((2, d)), (self.far_x, FX[d], d, h2))
            add(NY_[d], (FY[d],), (FY[d],) + blocks((d, 3), (d, 1)), (self.near_y, NY_[d], d, h1))
            add(NX_[d], (FX[d],), (FX[d],) + blocks((3, d), (1, d)), (self.near_x, NX_[d], d, h2))
        add(GX, (NY2,), (NY2,) + blocks((2, 0)), (self.far_x, GX, 0, h1))
        add(GY, (NX2,), (NX2,) + blocks((0, 2)), (self.far_y, GY, 0, h2))
        add(KX, (NY1, NY3, GX), (NY1, NY3, GX) + blocks((3, 0), (1, 0)), (self.near_x, KX, 0, h1))
        add(KY, (NX1, NX3, GY), (NX1, NX3, GY) + blocks((0, 3), (0, 1)), (self.near_y, KY, 0, h2))
        add(S0, (), (PH,), (self.swap, S0, 4, 4))
        add(S1, (), (PL,), (self.swap, S1, 6, 4))
        add(RC, (S0,), (S0, OH), (self.ship_text, RC, ZP2, 4, 0, HALF))
        add(RD, (S0,), (S0, OH), (self.ship_text, RD, ZM2, 4, HALF, HALF))
        add(RA3, (S0,), (S0, OH), (self.ring_back, RA3, 3, 5, 0))
        add(RB3, (S0,), (S0, OH), (self.ring_back, RB3, 3, 5, HALF))
        add(RA2, (S0, S1, RC, RA3), (S1, RC, RA3, OL), (self.ring_back, RA2, 2, 6, 0))
        add(RB2, (S0, S1, RD, RB3), (S1, RD, RB3, OL), (self.ring_back, RB2, 2, 6, HALF))
        add(RA1, (RA2,), (RA2,), (self.ring_back, RA1, 1, 7, 0))
        add(RB1, (RB2,), (RB2,), (self.ring_back, RB1, 1, 7, HALF))
        add(END_IMAGE, (KX, KY, NY0, NX0), (KX, KY, NY0, NX0, I3), (self.finish, "image", (0, 0)))
        add(END_TEXT, (RA1, RB1), (RA1, RB1), (self.finish, "text", (0, 0)))

    def finish(self, kind, slot):
        self.run.finish(kind, self.row((kind, slot)), self.parts[kind, slot])


def position():
    blk = lax.axis_index("blk")
    row = lax.axis_index("row")
    return (blk // 2) % NX, (blk // (2 * NX)) * 2 + row // NZ, row % NZ, blk % 2


def device(here, step):
    x = (here[0] + step[0] + NX) % NX
    y = (here[1] + step[1] + NY) % NY
    z = (here[2] + step[2] + NZ) % NZ
    core = (here[3] + step[3]) % 2
    return (((y // 2) * NX + x) * 2 + core, (y % 2) * NZ + z)


def unit_of(values):
    norm_rows = jnp.sqrt(jnp.sum(values * values, axis=1, keepdims=True) + EPS)
    return values / norm_rows, norm_rows


def project_back(grad_hat, unit_rows, norm_rows):
    return (grad_hat - unit_rows * jnp.sum(unit_rows * grad_hat, axis=1, keepdims=True)) / norm_rows


def kernel(
    images, texts, scale, bias, image_hat_grad, text_hat_grad,
    image_hat, text_hat, image_acc, text_acc, coef, out_stage, in_stage, send_sem, recv_sem,
):
    here = position()
    barrier = pltpu.get_barrier_semaphore()
    for step in PARTNERS:
        pl.semaphore_signal(barrier, inc=1, device_id=device(here, step), device_id_type=MESH)
    scale_value = scale[0]
    bias_value = bias[0]
    buffers = {"image": image_hat, "text": text_hat, "out": out_stage, "in": in_stage}
    sums = {"image": image_acc, "text": text_acc}
    grads = {"image": image_hat_grad, "text": text_hat_grad}

    class Run:
        def __init__(self):
            self.rows = {}
            self.index = {}
            self.sent = [0, 0]

        def copy(self, name, phase, source, row, target, to_row, count, step):
            self.rows[name] = self.rows.get(name, 0) + count
            self.sent[phase] += count
            pltpu.make_async_remote_copy(
                src_ref=buffers[source].at[pl.ds(row, count)],
                dst_ref=buffers[target].at[pl.ds(to_row, count)],
                send_sem=send_sem.at[phase],
                recv_sem=recv_sem.at[self.index.setdefault(name, len(self.index))],
                device_id=device(here, step),
                device_id_type=MESH,
            ).start()

        def whole(self, rows, phase, name):
            return pltpu.make_async_remote_copy(
                src_ref=out_stage.at[pl.ds(0, rows)],
                dst_ref=in_stage.at[pl.ds(0, rows)],
                send_sem=send_sem.at[phase],
                recv_sem=recv_sem.at[self.index[name]],
                device_id=device(here, CORE),
                device_id_type=MESH,
            )

        def wait(self, *names):
            for name in names:
                self.whole(self.rows[name], 0, name).wait_recv()

        def wait_sent(self):
            for phase, rows in enumerate(self.sent):
                if rows:
                    self.whole(rows, phase, X1).wait_send()

        def coef(self, block, start):
            rows, cols = pl.ds(block * BLOCK, BLOCK), pl.ds(start, BLOCK)
            dots = lax.dot_general(image_hat[rows], text_hat[cols], NT, preferred_element_type=F32)
            logits = scale_value * dots + bias_value
            coef[rows, cols] = (scale_value * jax.nn.sigmoid(logits)).astype(BF16)
            top, left = OWN_IMAGE - block * BLOCK, OWN_TEXT - start
            if 0 <= top < BLOCK and 0 <= left < BLOCK:
                base = left // LANES * LANES
                pairs = logits[top : top + ROWS, base : base + LANES]
                row = lax.broadcasted_iota(jnp.int32, pairs.shape, 0)
                col = lax.broadcasted_iota(jnp.int32, pairs.shape, 1)
                sign = jnp.where(col - row == left - base, 1.0, -1.0).astype(F32)
                coef[pl.ds(OWN_IMAGE, ROWS), pl.ds(start + base, LANES)] = (
                    -scale_value * sign * jax.nn.sigmoid(-sign * pairs)
                ).astype(BF16)

        def images(self, block):
            rows = pl.ds(block * BLOCK, BLOCK)
            image_acc[rows] = lax.dot_general(coef[rows], text_hat[...], NN, preferred_element_type=F32)

        def texts(self, start):
            rows = pl.ds(start, BLOCK)
            text_acc[rows] = lax.dot_general(coef[:, rows], image_hat[...], TN, preferred_element_type=F32)

        def total(self, kind, row, parts, first, count):
            value = sums[kind][pl.ds(row + first, count)]
            for begin, size, at in parts:
                if begin <= first and first + count <= begin + size:
                    value = value + in_stage[pl.ds(at + first - begin, count)].astype(F32)
            return value

        def stage(self, kind, row, parts, start, count, at):
            step = QUAR if parts else min(count, ROWS)
            for first in range(start, start + count, step):
                value = self.total(kind, row, parts, first, step)
                out_stage[pl.ds(at + first - start, step)] = value.astype(BF16)

        def finish(self, kind, row, parts):
            for first in (0, HALF):
                grads[kind][pl.ds(first, HALF)] = self.total(kind, row, parts, first, HALF)

    run = Run()
    plan = Plan(run)
    image_hat[pl.ds(OWN_IMAGE, ROWS)] = unit_of(images[...])[0].astype(BF16)
    text_hat[pl.ds(OWN_TEXT, ROWS)] = unit_of(texts[...])[0].astype(BF16)
    pl.semaphore_wait(barrier, len(PARTNERS))
    plan.execute(ORDER)
    run.wait_sent()


def body(images, texts, scale, bias):
    width = images.shape[1]
    vmem = pl.BlockSpec(memory_space=pltpu.VMEM)
    smem = pl.BlockSpec(memory_space=pltpu.SMEM)
    shard = jax.ShapeDtypeStruct(images.shape, F32)
    image_hat_grad, text_hat_grad = pl.pallas_call(
        kernel,
        out_shape=(shard, shard),
        in_specs=[vmem, vmem, smem, smem],
        out_specs=(vmem, vmem),
        scratch_shapes=[
            pltpu.VMEM((NI, width), BF16),
            pltpu.VMEM((NTX, width), BF16),
            pltpu.VMEM((NI, width), F32),
            pltpu.VMEM((NTX, width), F32),
            pltpu.VMEM((NI, NTX), BF16),
            pltpu.VMEM((STAGE, width), BF16),
            pltpu.VMEM((STAGE, width), BF16),
            pltpu.SemaphoreType.DMA((2,)),
            pltpu.SemaphoreType.DMA((GROUPS,)),
        ],
        compiler_params=pltpu.CompilerParams(
            collective_id=0, has_side_effects=True, vmem_limit_bytes=48 * 2**20
        ),
    )(images, texts, scale, bias)
    return project_back(image_hat_grad, *unit_of(images)), project_back(text_hat_grad, *unit_of(texts))


def solution(mesh):
    placed = (P(("blk", "row"), None), P(("blk", "row"), None), P(), P())
    return jax.shard_map(
        body,
        mesh=mesh,
        in_specs=placed,
        out_specs=(P(("blk", "row"), None), P(("blk", "row"), None)),
        check_vma=False,
    )
```

time: 400 us -> 54 us (0.14)
  the two profiles are of different devices: /device:TPU:8 before, /device:TPU:1 now
where the time goes in v2:
time: 54 us; the launch traced here: 53.9 us
  Pallas kernels  49.2 us (91%)
  other arithmetic  2.67 us (5%)
  between operations  2.02 us (4%)
    pallas_call x1, Pallas kernels, body(): pl.pallas_call(kernel, out_shape=(shard, shard), in_specs=[vmem, vmem, sm...  49.2 us
    reduce_sum x2, other arithmetic, unit_of(): norm_rows = jnp.sqrt(jnp.sum(values * values, axis=1, keepdims=True) + EPS)  1.27 us

profile of v2, /device:TPU:1, one launch (start us, length us, event | category | flops | bytes accessed | tf_op | source)
XLA Modules:
  0.0 53.9 jit_solution(11470477234818189739)
XLA Ops:
  0.6 0.0 copy-start.1
  2.0 0.0 copy-start
  2.0 1.1 %multiply_reduce_fusion.3 = f32[64]{0:T(128)S(1)} fusion(f32[64,1152]{1,0:T(8,128)} %images.1), kind=kLoop, calls=%fused_computation.5 | loop fusion | flops 147392 | bytes 295168 | tf_op jit(solution)/shard_map/reduce_sum | solution.py:276
  3.1 0.0 copy-done.1
  3.2 0.1 multiply_reduce_fusion.1
  3.3 0.0 copy-done
  3.3 49.2 %shard_map.59 = (f32[64,1152]{1,0:T(8,128)S(1)}, f32[64,1152]{1,0:T(8,128)S(1)}) custom-call(f32[64,1152]{1,0:T(8,128)S(1)} %copy-done, f32[64,1152]{1,0:T(8,128)S(1)} %copy-done.1, f32[1]{0:T(128)S(6)} %copy.6.scale, f32[1]{0:T(128)S(6)} %copy.7.bias), custom_call_target="tpu_custom_call" | custom-call | tf_op jit(solution)/shard_map/pallas_call | solution.py:390
  52.5 0.2 multiply_reduce_fusion.2
  52.7 0.2 multiply_reduce_fusion
  52.9 1.0 %subtract_divide_fusion = (f32[64,1152]{1,0:T(8,128)}, f32[64,1152]{1,0:T(8,128)}) fusion(f32[64,1152]{1,0:T(8,128)S(1)} %get-tuple-element.5, f32[64]{0:T(128)S(1)} %multiply_reduce_fusion, f32[64]{0:T(128)S(1)} %add_sqrt_fusion, f32[64,1152]{1,0:T(8,128)S(1)} %copy-done.1, f32[64,1152]{1,0:T(8,128)S(1)} %get-tuple-element.4, f32[64]{0:T(128)S(1)} %multiply_reduce_fusion.2, ...), kind=kLoop, calls=%fused_computation | loop fusion | flops 589824 | bytes 1770496 | tf_op jit(solution)/shard_map/div | solution.py:281
  (2 shorter events, 0.0 us)
Async XLA Ops:
  0.6 2.5 %copy-start.1 = (f32[64,1152]{1,0:T(8,128)S(1)}, f32[64,1152]{1,0:T(8,128)}, u32[]{:S(2)}) copy-start(f32[64,1152]{1,0:T(8,128)} %texts.1) | copy-start | bytes 884740
  2.0 1.3 %copy-start = (f32[64,1152]{1,0:T(8,128)S(1)}, f32[64,1152]{1,0:T(8,128)}, u32[]{:S(2)}) copy-start(f32[64,1152]{1,0:T(8,128)} %images.1) | copy-start | bytes 884740

commit v3 on v2

--- a/solution.py
+++ b/solution.py
@@ -55,11 +55,11 @@
 CPH, CPL = (CPH0, CPH1, CPH2, CPH3), (CPL0, CPL1, CPL2, CPL3)
 
 ORDER = (
-    ZA0, X1, Y2, ZB0, X2, Y1, Y1_1, ZA1, XD, X2_3, T0, YD, X2_1, Y1_3, ZB1, ZA2, T1, Y1_2, X2_2, T2, ZB2,
-    LY0, COL3, ZD, LX0, ZC, LX3, LY3, LY1, COL2, LX1, CPL3, LX2, LY2, T3, COL1, CPL2, CPL1, T4, COH2,
-    CPH0, CPH2, COL0, CPH3, CPH1, CPL0, COH0, I0, COH3, PH, S0, FY3, FX2, FY2, COH1, I1, OH, RD, RC, FY1,
-    FX1, FX3, NX2, RB3, NY2, FY0, I2, PL, S1, FX0, NY1, RA3, NX1, OL, NY3, RB2, GX, NX3, GY, RA2, I3, NX0,
-    NY0, RB1, KX, KY, RA1, END_IMAGE, END_TEXT,
+    Y2, X1, ZB0, X2, ZA0, Y1, X2_3, ZB1, Y1_1, YD, XD, Y1_3, ZA1, X2_1, T1, Y1_2, ZB2, X2_2, T0, LY0, LX0,
+    ZD, LX3, LY1, T2, ZC, LY3, COL2, CPL3, CPL2, ZA2, LX1, LY2, LX2, COL1, CPL1, T4, COL3, T3, COH2, COH3,
+    COH1, COH0, CPL0, CPH2, CPH0, CPH3, CPH1, PH, S0, COL0, OH, I0, RD, RB3, FY2, RC, FX2, I1, FY3, FX1,
+    PL, FX3, FY1, S1, NY2, NX2, I2, RA3, FY0, NX1, I3, FX0, NY1, OL, RB2, NX3, GX, GY, NY3, RA2, NX0, NY0,
+    RB1, KY, KX, RA1, END_IMAGE, END_TEXT,
 )
 
 

time: 54 us -> 53.1 us (0.983)
  Pallas kernels: 49.2 us -> 48.3 us
    pallas_call x1, Pallas kernels: 49.2 us -> 48.3 us  [body(): pl.pallas_call(kernel, out_shape=(shard, shard), in_specs=[vmem, vmem, sm...]
where the time goes in v3:
time: 53.1 us; the launch traced here: 52.9 us
  Pallas kernels  48.3 us (91%)
  other arithmetic  2.67 us (5%)
  between operations  2.02 us (4%)
    pallas_call x1, Pallas kernels, body(): pl.pallas_call(kernel, out_shape=(shard, shard), in_specs=[vmem, vmem, sm...  48.3 us
    reduce_sum x2, other arithmetic, unit_of(): norm_rows = jnp.sqrt(jnp.sum(values * values, axis=1, keepdims=True) + EPS)  1.27 us

profile of v3, /device:TPU:1, one launch (start us, length us, event | category | flops | bytes accessed | tf_op | source)
XLA Modules:
  0.0 52.9 jit_solution(9687523335049859862)
XLA Ops:
  0.6 0.0 copy-start.1
  2.0 0.0 copy-start
  2.0 1.1 %multiply_reduce_fusion.3 = f32[64]{0:T(128)S(1)} fusion(f32[64,1152]{1,0:T(8,128)} %images.1), kind=kLoop, calls=%fused_computation.5 | loop fusion | flops 147392 | bytes 295168 | tf_op jit(solution)/shard_map/reduce_sum | solution.py:276
  3.1 0.0 copy-done.1
  3.2 0.1 multiply_reduce_fusion.1
  3.3 0.0 copy-done
  3.3 48.3 %shard_map.59 = (f32[64,1152]{1,0:T(8,128)S(1)}, f32[64,1152]{1,0:T(8,128)S(1)}) custom-call(f32[64,1152]{1,0:T(8,128)S(1)} %copy-done, f32[64,1152]{1,0:T(8,128)S(1)} %copy-done.1, f32[1]{0:T(128)S(6)} %copy.6.scale, f32[1]{0:T(128)S(6)} %copy.7.bias), custom_call_target="tpu_custom_call" | custom-call | tf_op jit(solution)/shard_map/pallas_call | solution.py:390
  51.6 0.2 multiply_reduce_fusion.2
  51.8 0.2 multiply_reduce_fusion
  52.0 1.0 %subtract_divide_fusion = (f32[64,1152]{1,0:T(8,128)}, f32[64,1152]{1,0:T(8,128)}) fusion(f32[64,1152]{1,0:T(8,128)S(1)} %get-tuple-element.5, f32[64]{0:T(128)S(1)} %multiply_reduce_fusion, f32[64]{0:T(128)S(1)} %add_sqrt_fusion, f32[64,1152]{1,0:T(8,128)S(1)} %copy-done.1, f32[64,1152]{1,0:T(8,128)S(1)} %get-tuple-element.4, f32[64]{0:T(128)S(1)} %multiply_reduce_fusion.2, ...), kind=kLoop, calls=%fused_computation | loop fusion | flops 589824 | bytes 1770496 | tf_op jit(solution)/shard_map/div | solution.py:281
  (2 shorter events, 0.0 us)
Async XLA Ops:
  0.6 2.5 %copy-start.1 = (f32[64,1152]{1,0:T(8,128)S(1)}, f32[64,1152]{1,0:T(8,128)}, u32[]{:S(2)}) copy-start(f32[64,1152]{1,0:T(8,128)} %texts.1) | copy-start | bytes 884740
  2.0 1.3 %copy-start = (f32[64,1152]{1,0:T(8,128)S(1)}, f32[64,1152]{1,0:T(8,128)}, u32[]{:S(2)}) copy-start(f32[64,1152]{1,0:T(8,128)} %images.1) | copy-start | bytes 884740

commit v4 on v2

--- a/solution.py
+++ b/solution.py
@@ -40,7 +40,7 @@
 OWN_HI, OWN_LO, OTHER_HI, OTHER_LO = 0, BLOCK, NTH, NTH + BLOCK
 OWN_IMAGE, OWN_TEXT = IMAGE_ROW[0, 0], TEXT_ROW[0, 0]
 STAGE = 2176
-GROUPS = 64
+GROUPS = 56
 (
     X1, X2, Y1, Y2, XD, YD, Y1_1, Y1_2, Y1_3, X2_1, X2_2, X2_3, LY0, LY1, LY2, LY3, LX0, LX1, LX2,
     LX3, ZA0, ZA1, ZA2, ZB0, ZB1, ZB2, ZC, ZD, T0, T1, T2, T3, T4, COH0, COH1, COH2, COH3, COL0, COL1,
@@ -55,10 +55,10 @@
 CPH, CPL = (CPH0, CPH1, CPH2, CPH3), (CPL0, CPL1, CPL2, CPL3)
 
 ORDER = (
-    ZA0, X1, Y2, ZB0, X2, Y1, Y1_1, ZA1, XD, X2_3, T0, YD, X2_1, Y1_3, ZB1, ZA2, T1, Y1_2, X2_2, T2, ZB2,
-    LY0, COL3, ZD, LX0, ZC, LX3, LY3, LY1, COL2, LX1, CPL3, LX2, LY2, T3, COL1, CPL2, CPL1, T4, COH2,
-    CPH0, CPH2, COL0, CPH3, CPH1, CPL0, COH0, I0, COH3, PH, S0, FY3, FX2, FY2, COH1, I1, OH, RD, RC, FY1,
-    FX1, FX3, NX2, RB3, NY2, FY0, I2, PL, S1, FX0, NY1, RA3, NX1, OL, NY3, RB2, GX, NX3, GY, RA2, I3, NX0,
+    ZB0, X1, Y2, X2, ZA0, Y1, ZB1, Y1_3, YD, Y1_1, XD, X2_3, ZA1, X2_1, T0, LX3, T1, ZB2, T2, X2_2, Y1_2,
+    LY3, ZA2, LX1, ZD, ZC, COL3, LY0, LX0, CPL3, LY1, LX2, LY2, CPL1, COL1, T3, COL2, CPL2, T4, COH3,
+    COH1, CPH0, CPH3, CPH2, CPH1, PH, S0, CPL0, COH2, COH0, COL0, I0, OH, RD, RB3, FY2, FX2, I1, FY1, FX0,
+    RC, FX3, RA3, FY0, FY3, FX1, PL, OL, NX2, S1, NY2, I2, NX3, NY1, I3, NX1, NY3, RB2, GX, GY, RA2, NX0,
     NY0, RB1, KX, KY, RA1, END_IMAGE, END_TEXT,
 )
 
@@ -272,18 +272,14 @@
     return (((y // 2) * NX + x) * 2 + core, (y % 2) * NZ + z)
 
 
-def unit_of(values):
-    norm_rows = jnp.sqrt(jnp.sum(values * values, axis=1, keepdims=True) + EPS)
-    return values / norm_rows, norm_rows
-
-
-def project_back(grad_hat, unit_rows, norm_rows):
-    return (grad_hat - unit_rows * jnp.sum(unit_rows * grad_hat, axis=1, keepdims=True)) / norm_rows
+def norm_of(values):
+    return jnp.sqrt(jnp.sum(values * values, axis=1, keepdims=True) + EPS)
 
 
 def kernel(
-    images, texts, scale, bias, image_hat_grad, text_hat_grad,
-    image_hat, text_hat, image_acc, text_acc, coef, out_stage, in_stage, send_sem, recv_sem,
+    images, texts, scale, bias, image_part, text_part,
+    image_hat, text_hat, image_acc, text_acc, coef, out_stage, in_stage,
+    image_unit, text_unit, send_sem, recv_sem,
 ):
     here = position()
     barrier = pltpu.get_barrier_semaphore()
@@ -293,7 +289,8 @@
     bias_value = bias[0]
     buffers = {"image": image_hat, "text": text_hat, "out": out_stage, "in": in_stage}
     sums = {"image": image_acc, "text": text_acc}
-    grads = {"image": image_hat_grad, "text": text_hat_grad}
+    units = {"image": image_unit, "text": text_unit}
+    grads = {"image": image_part, "text": text_part}
 
     class Run:
         def __init__(self):
@@ -371,12 +368,16 @@
 
         def finish(self, kind, row, parts):
             for first in (0, HALF):
-                grads[kind][pl.ds(first, HALF)] = self.total(kind, row, parts, first, HALF)
+                rows = pl.ds(first, HALF)
+                value, unit = self.total(kind, row, parts, first, HALF), units[kind][rows]
+                grads[kind][rows] = value - unit * jnp.sum(unit * value, axis=1, keepdims=True)
 
     run = Run()
     plan = Plan(run)
-    image_hat[pl.ds(OWN_IMAGE, ROWS)] = unit_of(images[...])[0].astype(BF16)
-    text_hat[pl.ds(OWN_TEXT, ROWS)] = unit_of(texts[...])[0].astype(BF16)
+    image_unit[...] = images[...] / norm_of(images[...])
+    image_hat[pl.ds(OWN_IMAGE, ROWS)] = image_unit[...].astype(BF16)
+    text_unit[...] = texts[...] / norm_of(texts[...])
+    text_hat[pl.ds(OWN_TEXT, ROWS)] = text_unit[...].astype(BF16)
     pl.semaphore_wait(barrier, len(PARTNERS))
     plan.execute(ORDER)
     run.wait_sent()
@@ -387,7 +388,7 @@
     vmem = pl.BlockSpec(memory_space=pltpu.VMEM)
     smem = pl.BlockSpec(memory_space=pltpu.SMEM)
     shard = jax.ShapeDtypeStruct(images.shape, F32)
-    image_hat_grad, text_hat_grad = pl.pallas_call(
+    image_part, text_part = pl.pallas_call(
         kernel,
         out_shape=(shard, shard),
         in_specs=[vmem, vmem, smem, smem],
@@ -400,6 +401,8 @@
             pltpu.VMEM((NI, NTX), BF16),
             pltpu.VMEM((STAGE, width), BF16),
             pltpu.VMEM((STAGE, width), BF16),
+            pltpu.VMEM((ROWS, width), F32),
+            pltpu.VMEM((ROWS, width), F32),
             pltpu.SemaphoreType.DMA((2,)),
             pltpu.SemaphoreType.DMA((GROUPS,)),
         ],
@@ -407,7 +410,7 @@
             collective_id=0, has_side_effects=True, vmem_limit_bytes=48 * 2**20
         ),
     )(images, texts, scale, bias)
-    return project_back(image_hat_grad, *unit_of(images)), project_back(text_hat_grad, *unit_of(texts))
+    return image_part / norm_of(images), text_part / norm_of(texts)
 
 
 def solution(mesh):

time: 54 us -> 52.1 us (0.965)
  Pallas kernels: 49.2 us -> 47.7 us
    pallas_call x1, Pallas kernels: 49.2 us -> 47.7 us  [body(): pl.pallas_call(kernel, out_shape=(shard, shard), in_specs=[vmem, vmem, sm...]
    reduce_sum x4 -> x2, other arithmetic: 1.67 us -> 1.27 us  [norm_of(): return jnp.sqrt(jnp.sum(values * values, axis=1, keepdims=True) + EPS)]
where the time goes in v4:
time: 52.1 us; the launch traced here: 51.9 us
  Pallas kernels  47.7 us (92%)
  other arithmetic  2.21 us (4%)
  between operations  2.02 us (4%)
    pallas_call x1, Pallas kernels, body(): pl.pallas_call(kernel, out_shape=(shard, shard), in_specs=[vmem, vmem, sm...  47.7 us
    reduce_sum x2, other arithmetic, norm_of(): return jnp.sqrt(jnp.sum(values * values, axis=1, keepdims=True) + EPS)  1.27 us

profile of v4, /device:TPU:1, one launch (start us, length us, event | category | flops | bytes accessed | tf_op | source)
XLA Modules:
  0.0 51.9 jit_solution(15792482195224516745)
XLA Ops:
  0.6 0.0 copy-start.1
  2.0 0.0 copy-start
  2.0 1.1 %multiply_reduce_fusion.1 = f32[64]{0:T(128)S(1)} fusion(f32[64,1152]{1,0:T(8,128)} %images.1), kind=kLoop, calls=%fused_computation.1 | loop fusion | flops 147392 | bytes 295168 | tf_op jit(solution)/shard_map/reduce_sum | solution.py:276
  3.1 0.0 copy-done.1
  3.2 0.1 multiply_reduce_fusion
  3.3 0.0 copy-done
  3.3 47.7 %shard_map.59 = (f32[64,1152]{1,0:T(8,128)S(1)}, f32[64,1152]{1,0:T(8,128)S(1)}) custom-call(f32[64,1152]{1,0:T(8,128)S(1)} %copy-done, f32[64,1152]{1,0:T(8,128)S(1)} %copy-done.1, f32[1]{0:T(128)S(6)} %copy.6.scale, f32[1]{0:T(128)S(6)} %copy.7.bias), custom_call_target="tpu_custom_call" | custom-call | tf_op jit(solution)/shard_map/pallas_call | solution.py:391
  51.0 0.9 %broadcast_divide_fusion = (f32[64,1152]{1,0:T(8,128)}, f32[64,1152]{1,0:T(8,128)}) fusion(f32[64,1152]{1,0:T(8,128)S(1)} %get-tuple-element.5, f32[64]{0:T(128)S(1)} %add_sqrt_fusion, f32[64,1152]{1,0:T(8,128)S(1)} %get-tuple-element.4, f32[64]{0:T(128)S(1)} %add_sqrt_fusion.1), kind=kLoop, calls=%fused_computation.2 | loop fusion | flops 147456 | bytes 1180160 | tf_op jit(solution)/shard_map/div | solution.py:413
  (2 shorter events, 0.0 us)
Async XLA Ops:
  0.6 2.5 %copy-start.1 = (f32[64,1152]{1,0:T(8,128)S(1)}, f32[64,1152]{1,0:T(8,128)}, u32[]{:S(2)}) copy-start(f32[64,1152]{1,0:T(8,128)} %texts.1) | copy-start | bytes 884740
  2.0 1.3 %copy-start = (f32[64,1152]{1,0:T(8,128)S(1)}, f32[64,1152]{1,0:T(8,128)}, u32[]{:S(2)}) copy-start(f32[64,1152]{1,0:T(8,128)} %images.1) | copy-start | bytes 884740

commit v5 on v4

--- a/solution.py
+++ b/solution.py
@@ -47,7 +47,8 @@
     COL2, COL3, CPH0, CPH1, CPH2, CPH3, CPL0, CPL1, CPL2, CPL3, I0, I1, I2, I3, OH, OL, PH, PL, S0,
     S1, FX0, FX1, FX2, FX3, FY0, FY1, FY2, FY3, NX0, NX1, NX2, NX3, NY0, NY1, NY2, NY3, GX, GY, KX,
     KY, RA1, RA2, RA3, RB1, RB2, RB3, RC, RD, END_IMAGE, END_TEXT, LA, LB, Z4,
-) = range(92)
+    NORM_IMAGES, NORM_TEXTS,
+) = range(94)
 Y1S, X2S = (Y1, Y1_1, Y1_2, Y1_3), (X2, X2_1, X2_2, X2_3)
 LX, LY, I = (LX0, LX1, LX2, LX3), (LY0, LY1, LY2, LY3), (I0, I1, I2, I3)
 FX, FY, NX_, NY_ = (FX0, FX1, FX2, FX3), (FY0, FY1, FY2, FY3), (NX0, NX1, NX2, NX3), (NY0, NY1, NY2, NY3)
@@ -55,11 +56,11 @@
 CPH, CPL = (CPH0, CPH1, CPH2, CPH3), (CPL0, CPL1, CPL2, CPL3)
 
 ORDER = (
-    ZB0, X1, Y2, X2, ZA0, Y1, ZB1, Y1_3, YD, Y1_1, XD, X2_3, ZA1, X2_1, T0, LX3, T1, ZB2, T2, X2_2, Y1_2,
-    LY3, ZA2, LX1, ZD, ZC, COL3, LY0, LX0, CPL3, LY1, LX2, LY2, CPL1, COL1, T3, COL2, CPL2, T4, COH3,
-    COH1, CPH0, CPH3, CPH2, CPH1, PH, S0, CPL0, COH2, COH0, COL0, I0, OH, RD, RB3, FY2, FX2, I1, FY1, FX0,
-    RC, FX3, RA3, FY0, FY3, FX1, PL, OL, NX2, S1, NY2, I2, NX3, NY1, I3, NX1, NY3, RB2, GX, GY, RA2, NX0,
-    NY0, RB1, KX, KY, RA1, END_IMAGE, END_TEXT,
+    NORM_IMAGES, X1, Y2, X2, Y1, NORM_TEXTS, ZB0, ZA0, ZB1, Y1_3, YD, Y1_1, XD, X2_3, ZA1, X2_1, T0, LX3,
+    T1, ZB2, T2, X2_2, Y1_2, LY3, ZA2, LX1, ZD, ZC, COL3, LY0, LX0, CPL3, LY1, LX2, LY2, CPL1, COL1, T3,
+    COL2, CPL2, T4, COH3, COH1, CPH0, CPH3, CPH2, CPH1, PH, S0, CPL0, COH2, COH0, COL0, I0, OH, RD, RB3,
+    FY2, FX2, I1, FY1, FX0, RC, FX3, RA3, FY0, FY3, FX1, PL, OL, NX2, S1, NY2, I2, NX3, NY1, I3, NX1, NY3,
+    RB2, GX, GY, RA2, NX0, NY0, RB1, KX, KY, RA1, END_IMAGE, END_TEXT,
 )
 
 
@@ -129,10 +130,12 @@
 
     def gather(self):
         add, h1, h2 = self.add, 0, HALF
-        add(X1, (), (), (self.both_x, X1, 0, h1))
-        add(X2, (), (), (self.both_x, X2, 0, h2))
-        add(Y1, (), (), (self.both_y, Y1, 0, h1))
-        add(Y2, (), (), (self.both_y, Y2, 0, h2))
+        add(NORM_IMAGES, (), (), (self.run.normalize, "image", OWN_IMAGE))
+        add(NORM_TEXTS, (), (), (self.run.normalize, "text", OWN_TEXT))
+        add(X1, (), (NORM_IMAGES,), (self.both_x, X1, 0, h1))
+        add(X2, (), (NORM_IMAGES,), (self.both_x, X2, 0, h2))
+        add(Y1, (), (NORM_IMAGES,), (self.both_y, Y1, 0, h1))
+        add(Y2, (), (NORM_IMAGES,), (self.both_y, Y2, 0, h2))
         add(XD, (X1,), (), (self.onward_x, XD, 0, h1))
         add(YD, (Y2,), (), (self.onward_y, YD, 0, h2))
         for d, far, near in ((3, X1, Y2), (1, X1, Y2), (2, XD, YD)):
@@ -141,15 +144,15 @@
         for d, group in enumerate((LA, LB, LB, LA)):
             add(LY[d], (Y1S[d],), (), (self.onward_y, group, d, h1))
             add(LX[d], (X2S[d],), (), (self.onward_x, group, d, h2))
-        add(ZA0, (), (), (self.ring, ZA0, 0, 0, 0))
-        add(ZB0, (), (), (self.ring, ZB0, 0, 0, HALF))
+        add(ZA0, (), (NORM_TEXTS,), (self.ring, ZA0, 0, 0, 0))
+        add(ZB0, (), (NORM_TEXTS,), (self.ring, ZB0, 0, 0, HALF))
         add(ZA1, (ZA0,), (), (self.ring, ZA1, 7, 1, 0))
         add(ZB1, (ZB0,), (), (self.ring, ZB1, 7, 1, HALF))
         add(ZA2, (ZA1,), (), (self.ring, ZA2, 6, 2, 0))
         add(ZB2, (ZB1,), (), (self.ring, ZB2, 6, 2, HALF))
         add(ZC, (ZA1,), (), (self.pass_text, Z4, ZP2, 6, 0, HALF))
         add(ZD, (ZB1,), (), (self.pass_text, Z4, ZM2, 2, HALF, HALF))
-        add(T0, (), (), (self.share, T0, 0, 1))
+        add(T0, (), (NORM_TEXTS,), (self.share, T0, 0, 1))
         add(T1, (ZA0, ZB0), (), (self.share, T1, 1, 2))
         add(T2, (ZA1, ZB1), (), (self.share, T2, 2, 2))
         add(T3, (ZA2, ZB2), (), (self.share, T3, 3, 2))
@@ -289,6 +292,7 @@
     bias_value = bias[0]
     buffers = {"image": image_hat, "text": text_hat, "out": out_stage, "in": in_stage}
     sums = {"image": image_acc, "text": text_acc}
+    raw = {"image": images, "text": texts}
     units = {"image": image_unit, "text": text_unit}
     grads = {"image": image_part, "text": text_part}
 
@@ -297,6 +301,10 @@
             self.rows = {}
             self.index = {}
             self.sent = [0, 0]
+
+        def normalize(self, kind, row):
+            units[kind][...] = raw[kind][...] / norm_of(raw[kind][...])
+            buffers[kind][pl.ds(row, ROWS)] = units[kind][...].astype(BF16)
 
         def copy(self, name, phase, source, row, target, to_row, count, step):
             self.rows[name] = self.rows.get(name, 0) + count
@@ -374,10 +382,6 @@
 
     run = Run()
     plan = Plan(run)
-    image_unit[...] = images[...] / norm_of(images[...])
-    image_hat[pl.ds(OWN_IMAGE, ROWS)] = image_unit[...].astype(BF16)
-    text_unit[...] = texts[...] / norm_of(texts[...])
-    text_hat[pl.ds(OWN_TEXT, ROWS)] = text_unit[...].astype(BF16)
     pl.semaphore_wait(barrier, len(PARTNERS))
     plan.execute(ORDER)
     run.wait_sent()

time: 52.1 us -> 52.3 us (level)
  no operation moved by 1% of the time
where the time goes in v5:
time: 52.3 us; the launch traced here: 52.2 us
  Pallas kernels  47.9 us (92%)
  other arithmetic  2.21 us (4%)
  between operations  2.02 us (4%)
    pallas_call x1, Pallas kernels, body(): pl.pallas_call(kernel, out_shape=(shard, shard), in_specs=[vmem, vmem, sm...  47.9 us
    reduce_sum x2, other arithmetic, norm_of(): return jnp.sqrt(jnp.sum(values * values, axis=1, keepdims=True) + EPS)  1.27 us

profile of v5, /device:TPU:1, one launch (start us, length us, event | category | flops | bytes accessed | tf_op | source)
XLA Modules:
  0.0 52.2 jit_solution(8994270717201725636)
XLA Ops:
  0.6 0.0 copy-start.1
  2.0 0.0 copy-start
  2.0 1.1 %multiply_reduce_fusion.1 = f32[64]{0:T(128)S(1)} fusion(f32[64,1152]{1,0:T(8,128)} %images.1), kind=kLoop, calls=%fused_computation.1 | loop fusion | flops 147392 | bytes 295168 | tf_op jit(solution)/shard_map/reduce_sum | solution.py:279
  3.1 0.0 copy-done.1
  3.2 0.1 multiply_reduce_fusion
  3.3 0.0 copy-done
  3.3 47.9 %shard_map.59 = (f32[64,1152]{1,0:T(8,128)S(1)}, f32[64,1152]{1,0:T(8,128)S(1)}) custom-call(f32[64,1152]{1,0:T(8,128)S(1)} %copy-done, f32[64,1152]{1,0:T(8,128)S(1)} %copy-done.1, f32[1]{0:T(128)S(6)} %copy.6.scale, f32[1]{0:T(128)S(6)} %copy.7.bias), custom_call_target="tpu_custom_call" | custom-call | tf_op jit(solution)/shard_map/pallas_call | solution.py:395
  51.2 0.9 %broadcast_divide_fusion = (f32[64,1152]{1,0:T(8,128)}, f32[64,1152]{1,0:T(8,128)}) fusion(f32[64,1152]{1,0:T(8,128)S(1)} %get-tuple-element.5, f32[64]{0:T(128)S(1)} %add_sqrt_fusion, f32[64,1152]{1,0:T(8,128)S(1)} %get-tuple-element.4, f32[64]{0:T(128)S(1)} %add_sqrt_fusion.1), kind=kLoop, calls=%fused_computation.2 | loop fusion | flops 147456 | bytes 1180160 | tf_op jit(solution)/shard_map/div | solution.py:417
  (2 shorter events, 0.0 us)
Async XLA Ops:
  0.6 2.5 %copy-start.1 = (f32[64,1152]{1,0:T(8,128)S(1)}, f32[64,1152]{1,0:T(8,128)}, u32[]{:S(2)}) copy-start(f32[64,1152]{1,0:T(8,128)} %texts.1) | copy-start | bytes 884740
  2.0 1.3 %copy-start = (f32[64,1152]{1,0:T(8,128)S(1)}, f32[64,1152]{1,0:T(8,128)}, u32[]{:S(2)}) copy-start(f32[64,1152]{1,0:T(8,128)} %images.1) | copy-start | bytes 884740
